TPU v7x, 512 devices: a whole 4x4x16 slice. The times are simulated.
512 devices in a mesh: seq: 128 (over z, x, core), grp: 4 (over y).
Axes of the slice: x: 4, y: 4, z: 16, core: 2. Of those that a mesh axis runs over, the one named last changes fastest.
Arguments:
- main_qkv: bfloat16 [49152, 3, 2560], P(('seq', 'grp')), may hold values from -6 to 6
- guide_qkv: bfloat16 [49152, 3, 768], P(('seq', 'grp')), may hold values from -6 to 6
- main_head: bfloat16 [2560, 64], P('grp'), may hold values from -2 to 2
- guide_head: bfloat16 [768, 64], replicated, may hold values from -3.5 to 3.5
- window_start: int32 [128], replicated, may hold values from 0 to 126, as said below
- timestep: int32 [1], replicated, may hold values from 0 to 999
Outputs:
- guided: float32 [49152, 64], P(('seq', 'grp'))
Inputs may be any that keep to these rules, and one draw needn't show every extreme that they name: window_start[t] is t - 1 or t, drawn for each tile.
All inputs are finite; a program needn't handle non-finite values.
Results may differ from a plain program's by a relative error of at most 0.0041.
Values may be sent and summed in bfloat16 or wider, within the bound.
No kernel may reach another device: no remote copies, remote signals or barrier semaphores. Data moves between devices by JAX's collectives and lax.ppermute only.
A program may use at most 64 MiB of HBM per device.

v0:
```python
import math

import jax
import jax.numpy as jnp
from jax import lax
from jax.sharding import PartitionSpec as P

GHEADS = 6
HD = 128
TILE = 384


def passed_along(block, axis, distance):
    devices = range(lax.axis_size(axis))
    route = [(i - distance, i) for i in devices if i - distance in devices]
    return lax.ppermute(block, axis, route)


def attend(query, key_rows, value_rows, heads):
    q_count = query.shape[0]
    k_count = key_rows.shape[0]
    head_size = query.shape[1] // heads
    q_heads = query.reshape(q_count, heads, head_size)
    k_heads = key_rows.reshape(k_count, heads, head_size)
    v_heads = value_rows.reshape(k_count, heads, head_size)
    scores = jnp.einsum("qhd,khd->hqk", q_heads, k_heads, preferred_element_type=jnp.float32) * (
        1.0 / math.sqrt(head_size)
    )
    row_max = jnp.max(scores, axis=-1, keepdims=True)
    lifted = jnp.exp(scores - row_max)
    row_sum = jnp.sum(lifted, axis=-1, keepdims=True)
    weights = (lifted / row_sum).astype(jnp.bfloat16)
    blended = jnp.einsum("hqk,khd->qhd", weights, v_heads, preferred_element_type=jnp.float32)
    return blended.reshape(q_count, heads * head_size).astype(jnp.bfloat16)


def body(main_qkv, guide_qkv, main_head, guide_head, window_start, timestep):
    seq_index = lax.axis_index("seq")
    grp_index = lax.axis_index("grp")
    grp_count = lax.axis_size("grp")
    tok_rows = main_qkv.shape[0]
    block_rows = tok_rows * grp_count
    tiles_here = block_rows // TILE
    first_tile = seq_index * tiles_here
    heads_here = main_head.shape[0] // HD
    shard_kv = main_qkv[:, 1:]
    moved_shards = []
    for shift_by in (1, -1):
        moved_shards.append(passed_along(shard_kv, "seq", shift_by))
    regrouped, before_block, after_block = (
        lax.all_to_all(main_qkv, "grp", split_axis=2, concat_axis=0, tiled=True),
        lax.all_to_all(moved_shards[0], "grp", split_axis=2, concat_axis=0, tiled=True),
        lax.all_to_all(moved_shards[1], "grp", split_axis=2, concat_axis=0, tiled=True),
    )
    main_kv = regrouped[:, 1:]
    main_ext = jnp.concatenate([before_block, main_kv, after_block], axis=0)
    main_queries = regrouped[:, 0]

    def main_tile(tile_pos):
        global_tile = first_tile + tile_pos
        window_pos = lax.dynamic_index_in_dim(window_start, global_tile, 0, keepdims=False)
        window_rows = lax.dynamic_slice_in_dim(
            main_ext, (window_pos - first_tile + 1) * TILE, 2 * TILE, 0
        )
        return attend(main_queries, window_rows[:, 0], window_rows[:, 1], heads_here)

    main_mixed = lax.map(main_tile, jnp.arange(tiles_here, dtype=jnp.int32)).reshape(
        block_rows, main_head.shape[0]
    )
    main_speed = lax.psum_scatter(
        jnp.dot(main_mixed, main_head, preferred_element_type=jnp.float32),
        "grp",
        scatter_dimension=0,
        tiled=True,
    )
    guide_kv = guide_qkv[:, 1:]
    guide_all = lax.all_gather(guide_kv, "grp", axis=0, tiled=True)
    guide_sides = []
    for shift_by, edge_rows in ((1, guide_all), (-1, guide_all)):
        guide_sides.append(passed_along(edge_rows, "seq", shift_by))
    guide_before = guide_sides[0]
    guide_after = guide_sides[1]
    guide_ext = jnp.concatenate([guide_before, guide_all, guide_after], axis=0)
    guide_queries = guide_qkv[:, 0]
    piece_rows = TILE // grp_count
    piece_total = tok_rows // piece_rows
    my_first = (seq_index * grp_count + grp_index) * tok_rows

    def guide_piece(piece_pos):
        global_tile = (my_first + piece_pos * piece_rows) // TILE
        window_pos = lax.dynamic_index_in_dim(window_start, global_tile, 0, keepdims=False)
        window_rows = lax.dynamic_slice_in_dim(
            guide_ext, (window_pos - first_tile + 1) * TILE, 2 * TILE, 0
        )
        return attend(guide_queries, window_rows[:, 0], window_rows[:, 1], GHEADS)

    guide_mixed = lax.map(guide_piece, jnp.arange(piece_total, dtype=jnp.int32)).reshape(
        tok_rows, guide_head.shape[0]
    )
    guide_speed = jnp.dot(guide_mixed, guide_head, preferred_element_type=jnp.float32)
    weight = 1.0 + 2.0 * timestep[0].astype(jnp.float32) / 999.0
    return guide_speed + weight * (main_speed - guide_speed)


def solution(mesh):
    in_specs = (
        P(("seq", "grp"), None, None),
        P(("seq", "grp"), None, None),
        P("grp", None),
        P(),
        P(),
        P(),
    )
    out_specs = P(("seq", "grp"), None)
    return jax.shard_map(body, mesh=mesh, in_specs=in_specs, out_specs=out_specs, check_vma=False)
```

profile of v0, /device:TPU:6, one launch (start us, length us, event | category | flops | bytes accessed | tf_op | source)
XLA Modules:
  0.0 171.0 jit_solution(7814162269604686922)
XLA Ops:
  6.5 4.9 %copy.69 = bf16[96,3,2560]{0,1,2:T(4,128)(2,1)} copy(bf16[96,3,2560]{2,0,1:T(8,128)(2,1)} %param.6) | data formatting | bytes 2949120 | tf_op args[0]
  11.5 4.5 %all-to-all-start.1 = ((bf16[96,3,2560]{0,1,2:T(4,128)(2,1)}), bf16[96,3,2560]{0,1,2:T(4,128)(2,1)S(1)}, u32[]{:S(2)}, u32[]{:S(2)}) async-start(bf16[96,3,2560]{0,1,2:T(4,128)(2,1)} %copy.69), calls=%async_computation.1 | async-start | bytes 5242880 | tf_op jit(solution)/shard_map/all_to_all | solution.py:51
  15.9 2.2 %slice.35 = bf16[96,2,2560]{2,0,1:T(8,128)(2,1)} slice(bf16[96,3,2560]{2,0,1:T(8,128)(2,1)} %param.6), slice={[0:96], [1:3], [0:2560]} | slice | bytes 1966080 | tf_op jit(solution)/shard_map/slice | solution.py:46
  18.2 1.9 %collective-permute-start.2 = (bf16[96,2,2560]{2,0,1:T(8,128)(2,1)}, bf16[96,2,2560]{2,0,1:T(8,128)(2,1)}, u32[]{:S(2)}, u32[]{:S(2)}) collective-permute-start(bf16[96,2,2560]{2,0,1:T(8,128)(2,1)} %slice.35), channel_id=1, source_target_pairs={{0,4},{4,8},{8,12},{12,16},{16,20},{20,24},{24,28},{28,32},{32,36}... | collective-permute-start | bytes 2949128 | tf_op jit(solution)/shard_map/ppermute | solution.py:16
  20.1 3.6 %collective-permute-start.3 = (bf16[96,2,2560]{2,0,1:T(8,128)(2,1)}, bf16[96,2,2560]{2,0,1:T(8,128)(2,1)}, u32[]{:S(2)}, u32[]{:S(2)}) collective-permute-start(bf16[96,2,2560]{2,0,1:T(8,128)(2,1)} %slice.35), channel_id=1, source_target_pairs={{4,0},{8,4},{12,8},{16,12},{20,16},{24,20},{28,24},{32,28},{36,32}... | collective-permute-start | bytes 2949128 | tf_op jit(solution)/shard_map/ppermute | solution.py:16
  23.7 10.2 %collective-permute-done.2 = bf16[96,2,2560]{2,0,1:T(8,128)(2,1)} collective-permute-done((bf16[96,2,2560]{2,0,1:T(8,128)(2,1)}, bf16[96,2,2560]{2,0,1:T(8,128)(2,1)}, u32[]{:S(2)}, u32[]{:S(2)}) %collective-permute-start.2) | collective-permute-done | bytes 983072 | tf_op jit(solution)/shard_map/ppermute | solution.py:16
  33.9 3.8 %copy.66 = bf16[96,2,2560]{0,1,2:T(2,128)(2,1)} copy(bf16[96,2,2560]{2,0,1:T(8,128)(2,1)} %collective-permute-done.2) | data formatting | bytes 1966080 | tf_op jit(solution)/shard_map/ppermute | solution.py:16
  37.7 10.2 %all-to-all-done.1 = bf16[96,3,2560]{0,1,2:T(4,128)(2,1)S(1)} async-done(((bf16[96,3,2560]{0,1,2:T(4,128)(2,1)}), bf16[96,3,2560]{0,1,2:T(4,128)(2,1)S(1)}, u32[]{:S(2)}, u32[]{:S(2)}) %all-to-all-start.1) | async-done | bytes 1474592 | tf_op jit(solution)/shard_map/all_to_all | solution.py:51
  47.9 4.3 %all-to-all-start = ((bf16[96,2,2560]{0,1,2:T(2,128)(2,1)}), bf16[96,2,2560]{0,1,2:T(2,128)(2,1)}, u32[]{:S(2)}, u32[]{:S(2)}) async-start(bf16[96,2,2560]{0,1,2:T(2,128)(2,1)} %copy.66), calls=%async_computation | async-start | bytes 2621440 | tf_op jit(solution)/shard_map/all_to_all | solution.py:52
  52.2 0.0 all-gather.2.cloned.1.call-start
  52.3 1.1 copy.92
  53.3 0.0 all-gather.2.cloned.1.call-update
  53.4 3.8 %copy.72 = bf16[96,2,2560]{0,1,2:T(2,128)(2,1)} copy(bf16[96,2,2560]{2,0,1:T(8,128)(2,1)} %collective-permute-done.3) | data formatting | bytes 1966080 | tf_op jit(solution)/shard_map/ppermute | solution.py:16
  57.2 12.1 %all-to-all-done = bf16[96,2,2560]{0,1,2:T(2,128)(2,1)} async-done(((bf16[96,2,2560]{0,1,2:T(2,128)(2,1)}), bf16[96,2,2560]{0,1,2:T(2,128)(2,1)}, u32[]{:S(2)}, u32[]{:S(2)}) %all-to-all-start) | async-done | bytes 983072 | tf_op jit(solution)/shard_map/all_to_all | solution.py:52
  69.2 4.3 %all-to-all-start.2 = ((bf16[96,2,2560]{0,1,2:T(2,128)(2,1)}), bf16[96,2,2560]{0,1,2:T(2,128)(2,1)}, u32[]{:S(2)}, u32[]{:S(2)}) async-start(bf16[96,2,2560]{0,1,2:T(2,128)(2,1)} %copy.72), calls=%async_computation.2 | async-start | bytes 2621440 | tf_op jit(solution)/shard_map/all_to_all | solution.py:53
  73.6 0.0 reduce-scatter.4.cloned.1.call-start
  73.7 0.7 fusion.34
  75.0 3.1 %copy.71 = bf16[4,96,3,640]{3,1,0,2:T(8,128)(2,1)} copy(bf16[4,96,3,640]{1,2,3,0:T(4,128)(2,1)S(1)} %bitcast.65) | data formatting | bytes 2949120 | tf_op jit(solution)/shard_map/all_to_all | solution.py:51
  78.1 1.3 slice.42
  79.4 1.1 slice.45
  80.5 0.3 copy.77
  80.8 3.7 %copy.86 = bf16[96,2,4,640]{3,2,0,1:T(4,128)(2,1)S(1)} copy(bf16[96,2,4,640]{0,1,3,2:T(2,128)(2,1)} %bitcast.6) | data formatting | bytes 1966080 | tf_op jit(solution)/shard_map/all_to_all | solution.py:52
  84.5 0.1 copy.68
  84.6 14.6 %all-to-all-done.2 = bf16[96,2,2560]{0,1,2:T(2,128)(2,1)} async-done(((bf16[96,2,2560]{0,1,2:T(2,128)(2,1)}), bf16[96,2,2560]{0,1,2:T(2,128)(2,1)}, u32[]{:S(2)}, u32[]{:S(2)}) %all-to-all-start.2) | async-done | bytes 983072 | tf_op jit(solution)/shard_map/all_to_all | solution.py:53
  99.2 3.7 %copy.89 = bf16[96,2,4,640]{3,2,0,1:T(4,128)(2,1)S(1)} copy(bf16[96,2,4,640]{0,1,3,2:T(2,128)(2,1)} %bitcast.13) | data formatting | bytes 1966080 | tf_op jit(solution)/shard_map/all_to_all | solution.py:53
  102.9 0.1 copy.74
  103.0 2.3 %fusion.12 = bf16[768,2,640]{2,0,1:T(8,128)(2,1)S(1)} fusion(s32[]{:T(128)S(6)} %select_n.27, bf16[384,2,640]{2,0,1:T(8,128)(2,1)S(1)} %bitcast.69, bf16[384,2,640]{2,0,1:T(8,128)(2,1)S(1)} %slice.42, bf16[384,2,640]{2,0,1:T(8,128)(2,1)S(1)} %bitcast.70), kind=kLoop, calls=%fused_computation.19 | loop fusion | flops 5898240 | bytes 4915204 | tf_op jit(solution)/shard_map/concatenate | solution.py:56
  105.3 0.2 fusion.33
  105.4 1.3 copy.75
  106.8 0.6 copy.76
  107.4 4.5 %fusion.35 = (f32[5,384]{1,0:T(8,128)S(1)}, f32[5,384,768]{1,2,0:T(8,128)}) fusion(bf16[768,5,128]{0,2,1:T(8,128)(2,1)S(1)} %bitcast.75, bf16[384,5,128]{0,2,1:T(8,128)(2,1)S(1)} %bitcast.76), kind=kOutput, calls=%fused_computation.42 | convolution fusion | flops 381911808 | bytes 7380480 | tf_op jit(solution)/shard_map/while/body/eval_jaxpr/sub | solution.py:30
  111.9 3.6 %copy.59 = bf16[384,2,768]{0,2,1:T(8,128)(2,1)S(1)} copy(bf16[384,2,768]{2,1,0:T(2,128)(2,1)} %all-gather.2.cloned.1.call-done) | data formatting | bytes 2359296 | tf_op jit(solution)/shard_map/all_gather | solution.py:77
  115.5 1.9 %collective-permute-start = (bf16[384,2,768]{0,2,1:T(8,128)(2,1)S(1)}, bf16[384,2,768]{0,2,1:T(8,128)(2,1)S(1)}, u32[]{:S(2)}, u32[]{:S(2)}) collective-permute-start(bf16[384,2,768]{0,2,1:T(8,128)(2,1)S(1)} %copy.59), channel_id=1, source_target_pairs={{0,4},{4,8},{8,12},{12,16},{16,20},{20,24},{24,28},{28,32},{32,36}... | collective-permute-start | bytes 3538952 | tf_op jit(solution)/shard_map/ppermute | solution.py:16
  117.4 3.8 %collective-permute-start.1 = (bf16[384,2,768]{0,2,1:T(8,128)(2,1)S(1)}, bf16[384,2,768]{0,2,1:T(8,128)(2,1)}, u32[]{:S(2)}, u32[]{:S(2)}) collective-permute-start(bf16[384,2,768]{0,2,1:T(8,128)(2,1)S(1)} %copy.59), channel_id=1, source_target_pairs={{4,0},{8,4},{12,8},{16,12},{20,16},{24,20},{28,24},{32,28},{36,32}... | collective-permute-start | bytes 3538952 | tf_op jit(solution)/shard_map/ppermute | solution.py:16
  121.2 0.0 slice-start.1
  121.2 3.7 %fusion.18 = bf16[5,128,384]{2,1,0:T(8,128)(2,1)S(1)} fusion(bf16[768,5,128]{0,2,1:T(8,128)(2,1)} %bitcast.74, f32[5,384,768]{1,2,0:T(8,128)} %get-tuple-element.42, f32[5,384]{1,0:T(8,128)S(1)} %get-tuple-element.41), kind=kOutput, calls=%fused_computation.26 | convolution fusion | flops 380682240 | bytes 7380480 | tf_op jit(solution)/shard_map/while/body/eval_jaxpr/hqk,khd->qhd/dot_general | solution.py:33
  125.0 1.0 fusion.37
  126.0 0.0 reduce-scatter.4.cloned.1.call-update
  126.7 0.2 reshape_squeeze.8
  127.5 30.1 %reduce-scatter.4.cloned.1.call-done = f32[96,64]{1,0:T(8,128)} async-done(((f32[384,64]{1,0:T(8,128)}), f32[96,64]{1,0:T(8,128)}) %reduce-scatter.4.cloned.1.call-update) | async-done | bytes 24592
  157.6 0.9 copy.91
  158.5 0.0 collective-permute-done
  158.5 2.4 %fusion.10 = bf16[768,2,768]{0,2,1:T(8,128)(2,1)S(1)} fusion(s32[]{:T(128)S(6)} %select_n.25, bf16[384,2,768]{0,2,1:T(8,128)(2,1)S(1)} %collective-permute-done, bf16[384,2,768]{0,2,1:T(8,128)(2,1)S(1)} %copy.59, bf16[384,2,768]{0,2,1:T(8,128)(2,1)} %collective-permute-done.1), kind=kLoop, calls=%fused_computation.17 | loop fusion | flops 7077888 | bytes 5898244 | tf_op jit(solution)/shard_map/concatenate | solution.py:83
  160.8 0.2 fusion.32
  161.0 0.4 fusion.26
  161.4 1.4 fusion.36
  162.8 0.6 fusion.19
  163.4 0.8 multiply_add_fusion
  (12 shorter events, 0.0 us)
Async XLA Ops:
  6.5 156.8 %copy-start = (bf16[768,64]{0,1:T(8,128)(2,1)S(1)}, bf16[768,64]{0,1:T(8,128)(2,1)}, u32[]{:S(2)}) copy-start(bf16[768,64]{0,1:T(8,128)(2,1)} %param.9) | copy-start | bytes 294916
  11.5 36.4 %all-to-all-start.1 = ((bf16[96,3,2560]{0,1,2:T(4,128)(2,1)}), bf16[96,3,2560]{0,1,2:T(4,128)(2,1)S(1)}, u32[]{:S(2)}, u32[]{:S(2)}) async-start(bf16[96,3,2560]{0,1,2:T(4,128)(2,1)} %copy.69), calls=%async_computation.1 | async-start | bytes 5242880 | tf_op jit(solution)/shard_map/all_to_all | solution.py:51
  18.2 15.7 %collective-permute-start.2 = (bf16[96,2,2560]{2,0,1:T(8,128)(2,1)}, bf16[96,2,2560]{2,0,1:T(8,128)(2,1)}, u32[]{:S(2)}, u32[]{:S(2)}) collective-permute-start(bf16[96,2,2560]{2,0,1:T(8,128)(2,1)} %slice.35), channel_id=1, source_target_pairs={{0,4},{4,8},{8,12},{12,16},{16,20},{20,24},{24,28},{28,32},{32,36}... | collective-permute-start | bytes 2949128 | tf_op jit(solution)/shard_map/ppermute | solution.py:16
  20.1 33.3 %collective-permute-start.3 = (bf16[96,2,2560]{2,0,1:T(8,128)(2,1)}, bf16[96,2,2560]{2,0,1:T(8,128)(2,1)}, u32[]{:S(2)}, u32[]{:S(2)}) collective-permute-start(bf16[96,2,2560]{2,0,1:T(8,128)(2,1)} %slice.35), channel_id=1, source_target_pairs={{4,0},{8,4},{12,8},{16,12},{20,16},{24,20},{28,24},{32,28},{36,32}... | collective-permute-start | bytes 2949128 | tf_op jit(solution)/shard_map/ppermute | solution.py:16
  37.7 14.6 %slice-start = ((bf16[96,3,768]{2,0,1:T(8,128)(2,1)}), bf16[96,2,768]{2,0,1:T(8,128)(2,1)S(1)}, s32[]{:S(2)}) async-start(bf16[96,3,768]{2,0,1:T(8,128)(2,1)} %param.7), calls=%async_computation.6 | async-start | bytes 589824 | tf_op jit(solution)/shard_map/slice | solution.py:76
  47.9 21.4 %all-to-all-start = ((bf16[96,2,2560]{0,1,2:T(2,128)(2,1)}), bf16[96,2,2560]{0,1,2:T(2,128)(2,1)}, u32[]{:S(2)}, u32[]{:S(2)}) async-start(bf16[96,2,2560]{0,1,2:T(2,128)(2,1)} %copy.66), calls=%async_computation | async-start | bytes 2621440 | tf_op jit(solution)/shard_map/all_to_all | solution.py:52
  52.2 59.7 %all-gather.2.cloned.1.call-start = ((), (), s32[]{:S(2)}) async-start(), calls=%async_computation.4 | async-start | bytes 1474560 | tf_op jit(solution)/shard_map/all_gather | solution.py:77
  53.3 20.3 %copy-start.2 = (s32[128]{0:T(128)S(1)}, s32[128]{0:T(128)}, u32[]{:S(2)}) copy-start(s32[128]{0:T(128)} %param.10) | copy-start | bytes 1540
  69.2 29.9 %all-to-all-start.2 = ((bf16[96,2,2560]{0,1,2:T(2,128)(2,1)}), bf16[96,2,2560]{0,1,2:T(2,128)(2,1)}, u32[]{:S(2)}, u32[]{:S(2)}) async-start(bf16[96,2,2560]{0,1,2:T(2,128)(2,1)} %copy.72), calls=%async_computation.2 | async-start | bytes 2621440 | tf_op jit(solution)/shard_map/all_to_all | solution.py:53
  73.6 84.0 %reduce-scatter.4.cloned.1.call-start = ((), (), s32[]{:S(2)}) async-start(), calls=%async_computation.5 | async-start | bytes 245760
  115.5 43.0 %collective-permute-start = (bf16[384,2,768]{0,2,1:T(8,128)(2,1)S(1)}, bf16[384,2,768]{0,2,1:T(8,128)(2,1)S(1)}, u32[]{:S(2)}, u32[]{:S(2)}) collective-permute-start(bf16[384,2,768]{0,2,1:T(8,128)(2,1)S(1)} %copy.59), channel_id=1, source_target_pairs={{0,4},{4,8},{8,12},{12,16},{16,20},{20,24},{24,28},{28,32},{32,36}... | collective-permute-start | bytes 3538952 | tf_op jit(solution)/shard_map/ppermute | solution.py:16
  117.4 41.1 %collective-permute-start.1 = (bf16[384,2,768]{0,2,1:T(8,128)(2,1)S(1)}, bf16[384,2,768]{0,2,1:T(8,128)(2,1)}, u32[]{:S(2)}, u32[]{:S(2)}) collective-permute-start(bf16[384,2,768]{0,2,1:T(8,128)(2,1)S(1)} %copy.59), channel_id=1, source_target_pairs={{4,0},{8,4},{12,8},{16,12},{20,16},{24,20},{28,24},{32,28},{36,32}... | collective-permute-start | bytes 3538952 | tf_op jit(solution)/shard_map/ppermute | solution.py:16
  121.2 3.7 %copy-start.1 = (bf16[640,64]{0,1:T(8,128)(2,1)S(1)}, bf16[640,64]{0,1:T(8,128)(2,1)}, u32[]{:S(2)}) copy-start(bf16[640,64]{0,1:T(8,128)(2,1)} %param.8) | copy-start | bytes 245764
  121.2 5.4 %slice-start.1 = ((bf16[96,3,768]{2,0,1:T(8,128)(2,1)}), bf16[96,1,768]{2,0,1:T(8,128)(2,1)S(1)}, s32[]{:S(2)}) async-start(bf16[96,3,768]{2,0,1:T(8,128)(2,1)} %param.7), calls=%async_computation.7 | async-start | bytes 294912 | tf_op jit(solution)/shard_map/slice | solution.py:84
Sparse Core Ops, SparseCore 0:
  55.1 42.8 all-gather.1
  126.1 31.4 reduce-scatter.3
where the time goes:
time: 172 us; the launch traced here: 171 us
  waiting for transfers between devices  77.1 us (45%)
  local copies, waits for them, and re-layouts  36.8 us (21%)
  starting transfers between devices  24.4 us (14%)
  between operations  15.7 us (9%)
  matrix products  11 us (6%)
  other arithmetic  5.99 us (3%)
    unnamed x3, waiting for transfers between devices  30.1 us
    all_to_all x1, waiting for transfers between devices, body(): lax.all_to_all(moved_shards[1], 'grp', split_axis=2, concat_axis=0, tiled...  14.6 us
    all_to_all x1, waiting for transfers between devices, body(): lax.all_to_all(moved_shards[0], 'grp', split_axis=2, concat_axis=0, tiled...  12.1 us
    ppermute x4, starting transfers between devices, passed_along(): return lax.ppermute(block, axis, route)  11.3 us
    all_to_all x1, waiting for transfers between devices, body(): lax.all_to_all(main_qkv, 'grp', split_axis=2, concat_axis=0, tiled=True)  10.2 us
    ppermute x4, waiting for transfers between devices, passed_along(): return lax.ppermute(block, axis, route)  10.2 us
    ppermute x2, local copies, waits for them, and re-layouts, passed_along(): return lax.ppermute(block, axis, route)  7.6 us
    unnamed x9, local copies, waits for them, and re-layouts  6.89 us
  transfers between devices with their start and end apart: 9, of which 5 were waited for; matrix products, arithmetic and copies ran while one was open for 23% of the time, Pallas kernels for 0%

commit v1 on v0

v1 whole, which is shorter than its diff:
```python
import functools
import math

import jax
import jax.numpy as jnp
from jax import lax
from jax.experimental import pallas as pl
from jax.experimental.pallas import tpu as pltpu
from jax.sharding import PartitionSpec as P

HD = 128
TILE = 384
FIRST = 3
SCALE = 1.0 / math.sqrt(HD)
LIMIT = 24 * 1024 * 1024


def passed_along(block, axis, distance):
    devices = range(lax.axis_size(axis))
    route = [(i - distance, i) for i in devices if i - distance in devices]
    return lax.ppermute(block, axis, route)


def swapped(block):
    return lax.all_to_all(block, "grp", 0, 0)


def guide_pair(dst):
    return ((0, 1), (2, 1), (3, 4), (5, 4))[dst]


def pack(sources, groups, plan, rows):
    slabs = sorted({block[:2] for block in plan})

    def kernel(*refs):
        ins, out = refs[: len(sources)], refs[len(sources)]
        held, sem = refs[len(sources) + 1 : -1], refs[-1]
        copies = [
            pltpu.make_async_copy(ins[src].at[index], held[i], sem.at[i])
            for i, (src, index) in enumerate(slabs)
        ]
        for copy in copies:
            copy.start()
        for i, slab in enumerate(slabs):
            copies[i].wait()
            for src, index, row, count, head, group, at in plan:
                if (src, index) == slab:
                    out[group, pl.ds(at, count), :] = held[i][pl.ds(row, count), pl.ds(head * HD, HD)]

    return pl.pallas_call(
        kernel,
        out_shape=jax.ShapeDtypeStruct((groups, rows, HD), jnp.bfloat16),
        in_specs=[pl.BlockSpec(memory_space=pl.ANY)] * len(sources),
        out_specs=pl.BlockSpec(memory_space=pltpu.VMEM),
        scratch_shapes=[pltpu.VMEM(sources[src].shape[1:], jnp.bfloat16) for src, _ in slabs]
        + [pltpu.SemaphoreType.DMA((len(slabs),))],
        compiler_params=pltpu.CompilerParams(vmem_limit_bytes=LIMIT),
    )(*sources)


def head_mix(query, keys, values):
    scores = lax.dot_general(
        query, keys, (((1,), (1,)), ((), ())), preferred_element_type=jnp.float32
    )
    top = jnp.max(scores, axis=-1, keepdims=True)
    lifted = jnp.exp((scores - top) * SCALE)
    total = jnp.sum(lifted, axis=-1, keepdims=True)
    weights = (lifted * (1.0 / total)).astype(jnp.bfloat16)
    mixed = lax.dot_general(
        weights, values, (((1,), (0,)), ((), ())), preferred_element_type=jnp.float32
    )
    return mixed.astype(jnp.bfloat16)


def attention(side, half, weight, own, before, after, queries, main_head, guide_heads, earlier,
              heads, first_head, has_guide, tok):
    groups, rows, _ = own.shape
    q_rows = queries.shape[1]

    def kernel(side_ref, half_ref, weight_ref, own_ref, before_ref, after_ref, q_ref, wm_ref, wg_ref, earlier_ref,
               out_ref, kv, q_buf, mixed, sem):
        own_copy = pltpu.make_async_copy(own_ref, kv.at[0], sem.at[0])
        q_copy = pltpu.make_async_copy(q_ref, q_buf, sem.at[1])
        own_copy.start()
        q_copy.start()

        @pl.when(side_ref[0] == 0)
        def _():
            copy = pltpu.make_async_copy(before_ref, kv.at[1], sem.at[2])
            copy.start()
            copy.wait()

        @pl.when(side_ref[0] != 0)
        def _():
            copy = pltpu.make_async_copy(after_ref, kv.at[1], sem.at[2])
            copy.start()
            copy.wait()

        own_copy.wait()
        q_copy.wait()

        def window(block):
            return kv[:, :, pl.ds(block * tok, tok), :].reshape(2 * groups * tok, HD)

        for h in range(heads):
            query = q_buf[:, pl.ds((first_head + h) * tok, tok), :].reshape(groups * tok, HD)
            mixed[:, pl.ds(h * HD, HD)] = head_mix(query, window(2 * h), window(2 * h + 1))
        w = weight_ref[0]
        if has_guide:
            base = 2 * heads
            q_at = q_rows - tok - tok // 2
            query = q_buf[:, pl.ds(q_at, tok), :].reshape(groups * tok, HD)
            whole = head_mix(query, window(base), window(base + 1))
            query = q_buf[:, pl.ds(q_at + tok, tok // 2), :].reshape(groups * tok // 2, HD)
            shared = head_mix(query, window(base + 2), window(base + 3))
            shared = shared.reshape(groups, tok // 2, HD)
            blank = jnp.zeros_like(shared)
            upper = half_ref[0] != 0
            shared = jnp.concatenate(
                [jnp.where(upper, blank, shared), jnp.where(upper, shared, blank)], axis=1
            )
            whole = whole.reshape(groups, tok, HD)
        for j in range(groups):
            part = lax.dot_general(
                wm_ref[:, pl.ds(first_head * HD, heads * HD)], mixed[pl.ds(j * tok, tok), :],
                (((1,), (1,)), ((), ())), preferred_element_type=jnp.float32,
            ) * w
            if has_guide:
                side_by_side = jnp.concatenate([whole[j], shared[j]], axis=1)
                part += lax.dot_general(
                    wg_ref[...], side_by_side, (((1,), (1,)), ((), ())),
                    preferred_element_type=jnp.float32,
                ) * (1.0 - w)
                part += earlier_ref[j]
            out_ref[j] = part

    smem = pl.BlockSpec(memory_space=pltpu.SMEM)
    vmem = pl.BlockSpec(memory_space=pltpu.VMEM)
    anywhere = pl.BlockSpec(memory_space=pl.ANY)
    outc = main_head.shape[0]
    pairs = heads + (1.5 if has_guide else 0)
    flops = int(4 * pairs * groups * tok * 2 * groups * tok * HD)
    return pl.pallas_call(
        kernel,
        out_shape=jax.ShapeDtypeStruct((groups, outc, tok), jnp.float32),
        in_specs=[smem] * 3 + [anywhere] * 4 + [vmem] * 3,
        out_specs=vmem,
        scratch_shapes=[
            pltpu.VMEM((2, groups, rows, HD), jnp.bfloat16),
            pltpu.VMEM((groups, q_rows, HD), jnp.bfloat16),
            pltpu.VMEM((groups * tok, heads * HD), jnp.bfloat16),
            pltpu.SemaphoreType.DMA((3,)),
        ],
        compiler_params=pltpu.CompilerParams(vmem_limit_bytes=LIMIT),
        cost_estimate=pl.CostEstimate(flops=flops, bytes_accessed=4 * rows * groups * HD * 2, transcendentals=0),
    )(side, half, weight, own, before, after, queries, main_head, guide_heads, earlier)


def body(main_qkv, guide_qkv, main_head, guide_head, window_start, timestep):
    seq_index = lax.axis_index("seq")
    grp_index = lax.axis_index("grp")
    groups = lax.axis_size("grp")
    tok = main_qkv.shape[0]
    heads = main_head.shape[0] // HD
    assert groups * tok == TILE and window_start.shape[0] == lax.axis_size("seq")
    main = main_qkv.transpose(1, 0, 2)
    guide = guide_qkv.transpose(1, 0, 2)
    main_head = main_head.T
    guide_head = guide_head.T

    plan1, plan2, plan3 = [], [], []
    for g in range(groups):
        for h in range(heads):
            plan, at = (plan1, h) if h < FIRST else (plan2, h - FIRST)
            for kv in (0, 1):
                plan.append((0, 1 + kv, 0, tok, g * heads + h, g, (2 * at + kv) * tok))
            plan3.append((0, 0, 0, tok, g * heads + h, g, h * tok))
        whole, shared = guide_pair(g)
        base = 2 * (heads - FIRST)
        for i, (kv, head) in enumerate(((1, whole), (2, whole), (1, shared), (2, shared))):
            plan2.append((1, kv, 0, tok, head, g, (base + i) * tok))
        plan3.append((1, 0, 0, tok, whole, g, heads * tok))
        plan3.append((1, 0, (g % 2) * (tok // 2), tok // 2, shared, g, (heads + 1) * tok))
    own1 = swapped(pack([main], groups, plan1, 2 * FIRST * tok))
    own2 = swapped(pack([main, guide], groups, plan2, (2 * (heads - FIRST) + 4) * tok))
    queries = swapped(pack([main, guide], groups, plan3, (heads + 1) * tok + tok // 2))
    before1, after1 = passed_along(own1, "seq", 1), passed_along(own1, "seq", -1)
    before2, after2 = passed_along(own2, "seq", 1), passed_along(own2, "seq", -1)

    window_pos = lax.dynamic_slice_in_dim(window_start, seq_index, 1, 0)
    side = (window_pos == seq_index).astype(jnp.int32)
    half = (grp_index % 2).astype(jnp.int32).reshape(1)
    weight = 1.0 + 2.0 * timestep.astype(jnp.float32) / 999.0
    table = jnp.array([guide_pair(g) for g in range(groups)], jnp.int32)
    mine = lax.dynamic_index_in_dim(table, grp_index, 0, keepdims=False)
    guide_heads = jnp.concatenate(
        [lax.dynamic_slice_in_dim(guide_head, mine[i] * HD, HD, 1) for i in (0, 1)], axis=1
    )
    common = (main_head, guide_heads)
    nothing = jnp.zeros((1, 8, 128), jnp.float32)
    part = attention(side, half, weight, own1, before1, after1, queries, *common, nothing,
                     heads=FIRST, first_head=0, has_guide=False, tok=tok)
    part = attention(side, half, weight, own2, before2, after2, queries, *common, part,
                     heads=heads - FIRST, first_head=FIRST, has_guide=True, tok=tok)
    return jnp.sum(swapped(part), axis=0).T


def solution(mesh):
    in_specs = (
        P(("seq", "grp"), None, None),
        P(("seq", "grp"), None, None),
        P("grp", None),
        P(),
        P(),
        P(),
    )
    out_specs = P(("seq", "grp"), None)
    return jax.shard_map(body, mesh=mesh, in_specs=in_specs, out_specs=out_specs, check_vma=False)
```

time: 172 us -> 72 us (0.42)
  the two profiles are of different devices: /device:TPU:6 before, /device:TPU:384 now
where the time goes in v1:
time: 72 us; the launch traced here: 71.3 us
  starting transfers between devices  25.4 us (35%)
  waiting for transfers between devices  17.2 us (24%)
  Pallas kernels  11.9 us (17%)
  blocking collectives  8.36 us (12%)
  local copies, waits for them, and re-layouts  5.09 us (7%)
  between operations  2.74 us (4%)
    all_to_all x3, waiting for transfers between devices, swapped(): return lax.all_to_all(block, 'grp', 0, 0)  17.2 us
    ppermute x4, starting transfers between devices, passed_along(): return lax.ppermute(block, axis, route)  13 us
    all_to_all x3, starting transfers between devices, swapped(): return lax.all_to_all(block, 'grp', 0, 0)  12.4 us
    all_to_all x1, blocking collectives, swapped(): return lax.all_to_all(block, 'grp', 0, 0)  8.36 us
    pallas_call x2, Pallas kernels, attention(): pl.pallas_call(kernel, out_shape=jax.ShapeDtypeStruct((groups, outc, tok)...  6.77 us
    pallas_call x3, Pallas kernels, pack(): pl.pallas_call(kernel, out_shape=jax.ShapeDtypeStruct((groups, rows, HD),...  5.15 us
    unnamed x12, local copies, waits for them, and re-layouts  2.41 us
  transfers between devices with their start and end apart: 7, of which 3 were waited for; matrix products, arithmetic and copies ran while one was open for 4% of the time, Pallas kernels for 9%

profile of v1, /device:TPU:384, one launch (start us, length us, event | category | flops | bytes accessed | tf_op | source)
XLA Modules:
  0.0 71.3 jit_solution(16632162842317873751)
XLA Ops:
  0.0 0.0 copy-start
  0.0 1.4 %copy-done = bf16[96,3,2560]{2,0,1:T(8,128)(2,1)S(1)} copy-done((bf16[96,3,2560]{2,0,1:T(8,128)(2,1)S(1)}, bf16[96,3,2560]{2,0,1:T(8,128)(2,1)}, u32[]{:S(2)}) %copy-start) | copy-done | bytes 1474584
  1.4 0.0 copy-start.2
  1.4 1.0 %copy-done.2 = bf16[96,3,768]{2,0,1:T(8,128)(2,1)S(1)} copy-done((bf16[96,3,768]{2,0,1:T(8,128)(2,1)S(1)}, bf16[96,3,768]{2,0,1:T(8,128)(2,1)}, u32[]{:S(2)}) %copy-start.2) | copy-done | bytes 442392
  2.4 0.0 copy-start.1
  2.4 2.1 %shard_map.73 = bf16[4,768,128]{2,1,0:T(8,128)(2,1)} custom-call(bf16[3,96,2560]{2,1,0:T(8,128)(2,1)S(1)} %bitcast.12, bf16[3,96,768]{2,1,0:T(8,128)(2,1)S(1)} %bitcast.15), custom_call_target="tpu_custom_call" | custom-call | tf_op jit(solution)/shard_map/pallas_call | solution.py:50
  4.5 4.5 %all-to-all-start = ((bf16[4,768,128]{2,1,0:T(8,128)(2,1)}), bf16[4,768,128]{2,1,0:T(8,128)(2,1)S(1)}, u32[]{:S(2)}, u32[]{:S(2)}) async-start(bf16[4,768,128]{2,1,0:T(8,128)(2,1)} %shard_map.73), calls=%async_computation | async-start | bytes 1572864 | tf_op jit(solution)/shard_map/all_to_all | solution.py:25
  8.9 0.0 copy-done.1
  9.0 0.0 copy-start.3
  9.0 1.6 %shard_map.75 = bf16[4,576,128]{2,1,0:T(8,128)(2,1)} custom-call(bf16[3,96,2560]{2,1,0:T(8,128)(2,1)S(1)} %bitcast.13), custom_call_target="tpu_custom_call" | custom-call | tf_op jit(solution)/shard_map/pallas_call | solution.py:50
  10.6 10.7 %all-to-all-done.own_ref = bf16[4,768,128]{2,1,0:T(8,128)(2,1)S(1)} async-done(((bf16[4,768,128]{2,1,0:T(8,128)(2,1)}), bf16[4,768,128]{2,1,0:T(8,128)(2,1)S(1)}, u32[]{:S(2)}, u32[]{:S(2)}) %all-to-all-start) | async-done | bytes 786464 | tf_op jit(solution)/shard_map/all_to_all | solution.py:25
  21.2 3.5 %all-to-all-start.2 = ((bf16[4,576,128]{2,1,0:T(8,128)(2,1)}), bf16[4,576,128]{2,1,0:T(8,128)(2,1)S(1)}, u32[]{:S(2)}, u32[]{:S(2)}) async-start(bf16[4,576,128]{2,1,0:T(8,128)(2,1)} %shard_map.75), calls=%async_computation.2 | async-start | bytes 1179648 | tf_op jit(solution)/shard_map/all_to_all | solution.py:25
  24.7 0.0 copy-start.5
  24.7 0.0 copy-start.4
  24.7 4.7 %collective-permute-start.1 = (bf16[4,768,128]{2,1,0:T(8,128)(2,1)S(1)}, bf16[4,768,128]{2,1,0:T(8,128)(2,1)}, u32[]{:S(2)}, u32[]{:S(2)}) collective-permute-start(bf16[4,768,128]{2,1,0:T(8,128)(2,1)S(1)} %all-to-all-done.own_ref), channel_id=1, source_target_pairs={{4,0},{8,4},{12,8},{16,12},{20,16},{24,20},{28,24},{32,28},{36,32}... | collective-permute-start | bytes 2359304 | tf_op jit(solution)/shard_map/ppermute | solution.py:21
  29.5 1.9 %collective-permute-start = (bf16[4,768,128]{2,1,0:T(8,128)(2,1)S(1)}, bf16[4,768,128]{2,1,0:T(8,128)(2,1)}, u32[]{:S(2)}, u32[]{:S(2)}) collective-permute-start(bf16[4,768,128]{2,1,0:T(8,128)(2,1)S(1)} %all-to-all-done.own_ref), channel_id=1, source_target_pairs={{0,4},{4,8},{8,12},{12,16},{16,20},{20,24},{24,28},{28,32},{32,36}... | collective-permute-start | bytes 2359304 | tf_op jit(solution)/shard_map/ppermute | solution.py:21
  31.4 2.6 %all-to-all-done.2.own_ref = bf16[4,576,128]{2,1,0:T(8,128)(2,1)S(1)} async-done(((bf16[4,576,128]{2,1,0:T(8,128)(2,1)}), bf16[4,576,128]{2,1,0:T(8,128)(2,1)S(1)}, u32[]{:S(2)}, u32[]{:S(2)}) %all-to-all-start.2) | async-done | bytes 589856 | tf_op jit(solution)/shard_map/all_to_all | solution.py:25
  34.0 4.4 %collective-permute-start.3 = (bf16[4,576,128]{2,1,0:T(8,128)(2,1)S(1)}, bf16[4,576,128]{2,1,0:T(8,128)(2,1)}, u32[]{:S(2)}, u32[]{:S(2)}) collective-permute-start(bf16[4,576,128]{2,1,0:T(8,128)(2,1)S(1)} %all-to-all-done.2.own_ref), channel_id=1, source_target_pairs={{4,0},{8,4},{12,8},{16,12},{20,16},{24,20},{28,24},{32,28},{36,32}... | collective-permute-start | bytes 1769480 | tf_op jit(solution)/shard_map/ppermute | solution.py:21
  38.4 1.9 %collective-permute-start.2 = (bf16[4,576,128]{2,1,0:T(8,128)(2,1)S(1)}, bf16[4,576,128]{2,1,0:T(8,128)(2,1)}, u32[]{:S(2)}, u32[]{:S(2)}) collective-permute-start(bf16[4,576,128]{2,1,0:T(8,128)(2,1)S(1)} %all-to-all-done.2.own_ref), channel_id=1, source_target_pairs={{0,4},{4,8},{8,12},{12,16},{16,20},{20,24},{24,28},{28,32},{32,36}... | collective-permute-start | bytes 1769480 | tf_op jit(solution)/shard_map/ppermute | solution.py:21
  40.3 0.0 copy-done.3
  40.3 1.5 %shard_map.74 = bf16[4,624,128]{2,1,0:T(8,128)(2,1)} custom-call(bf16[3,96,2560]{2,1,0:T(8,128)(2,1)S(1)} %bitcast.14, bf16[3,96,768]{2,1,0:T(8,128)(2,1)S(1)} %bitcast.16), custom_call_target="tpu_custom_call" | custom-call | tf_op jit(solution)/shard_map/pallas_call | solution.py:50
  41.8 4.5 %all-to-all-start.1 = ((bf16[4,624,128]{2,1,0:T(8,128)(2,1)}), bf16[4,624,128]{2,1,0:T(8,128)(2,1)S(1)}, u32[]{:S(2)}, u32[]{:S(2)}) async-start(bf16[4,624,128]{2,1,0:T(8,128)(2,1)} %shard_map.74), calls=%async_computation.1 | async-start | bytes 1277952 | tf_op jit(solution)/shard_map/all_to_all | solution.py:25
  46.3 0.7 constant_dynamic-slice_fusion
  46.9 0.6 fusion
  49.4 0.0 copy-done.5
  49.4 0.7 dynamic_slice.13
  50.8 0.7 %dynamic-slice_bitcast_fusion.1 = (bf16[64,128]{1,0:T(8,128)(2,1)S(1)}, bf16[64,128]{1,0:T(8,128)(2,1)S(1)}) fusion(bf16[768,64]{0,1:T(8,128)(2,1)} %param.10, s32[]{:T(128)S(6)} %select_n.23, s32[]{:T(128)S(6)} %select_n.24), kind=kLoop, calls=%fused_computation.2 | loop fusion | bytes 65544 | tf_op jit(solution)/shard_map/dynamic_slice | solution.py:197
  51.5 4.0 %all-to-all-done.1.q_ref = bf16[4,624,128]{2,1,0:T(8,128)(2,1)S(1)} async-done(((bf16[4,624,128]{2,1,0:T(8,128)(2,1)}), bf16[4,624,128]{2,1,0:T(8,128)(2,1)S(1)}, u32[]{:S(2)}, u32[]{:S(2)}) %all-to-all-start.1) | async-done | bytes 639008 | tf_op jit(solution)/shard_map/all_to_all | solution.py:25
  55.5 0.0 collective-permute-done.3.after_ref
  55.5 0.0 collective-permute-done.2.before_ref
  55.5 0.0 copy-done.4
  55.5 3.3 %shard_map.76.earlier_ref = f32[4,64,96]{2,1,0:T(8,128)S(1)} custom-call(s32[1]{0:T(128)S(6)} %convert_element_type.6.side_ref, s32[1]{0:T(128)} %bitcast.1.half_ref, f32[1]{0:T(128)S(6)} %add.22.weight_ref, bf16[4,576,128]{2,1,0:T(8,128)(2,1)S(1)} %all-to-all-done.2.own_ref, bf16[4,576,128]{2,1,0:T(8,128)(2,1)} %collective-permute-done.2.before_ref, ...), custom_call_target="tpu_custom_call" | custom-call | flops 452984832 | bytes 2359296 | tf_op jit(solution)/shard_map/pallas_call | solution.py:143
  58.9 0.0 collective-permute-done.1.after_ref
  58.9 0.0 collective-permute-done.before_ref
  58.9 3.4 %shard_map.77 = f32[4,64,96]{2,1,0:T(8,128)S(1)} custom-call(s32[1]{0:T(128)S(6)} %convert_element_type.6.side_ref, s32[1]{0:T(128)} %bitcast.1.half_ref, f32[1]{0:T(128)S(6)} %add.22.weight_ref, bf16[4,768,128]{2,1,0:T(8,128)(2,1)S(1)} %all-to-all-done.own_ref, bf16[4,768,128]{2,1,0:T(8,128)(2,1)} %collective-permute-done.before_ref, ...), custom_call_target="tpu_custom_call" | custom-call | flops 528482304 | bytes 3145728 | tf_op jit(solution)/shard_map/pallas_call | solution.py:143
  62.3 8.4 %all_to_all.20 = f32[4,64,96]{2,1,0:T(8,128)S(1)} all-to-all(f32[4,64,96]{2,1,0:T(8,128)S(1)} %shard_map.77), channel_id=1, replica_groups=mesh['seq'=128,'grp'=4] {'grp'}, dimensions={0} | all-to-all | bytes 196608 | tf_op jit(solution)/shard_map/all_to_all | solution.py:25
  70.7 0.6 reduce_sum.9
  (2 shorter events, 0.0 us)
Async XLA Ops:
  0.0 1.4 %copy-start = (bf16[96,3,2560]{2,0,1:T(8,128)(2,1)S(1)}, bf16[96,3,2560]{2,0,1:T(8,128)(2,1)}, u32[]{:S(2)}) copy-start(bf16[96,3,2560]{2,0,1:T(8,128)(2,1)} %param.7) | copy-start | bytes 4423684
  1.4 1.0 %copy-start.2 = (bf16[96,3,768]{2,0,1:T(8,128)(2,1)S(1)}, bf16[96,3,768]{2,0,1:T(8,128)(2,1)}, u32[]{:S(2)}) copy-start(bf16[96,3,768]{2,0,1:T(8,128)(2,1)} %param.8) | copy-start | bytes 1327108
  2.4 6.6 %copy-start.1 = (bf16[96,3,2560]{2,0,1:T(8,128)(2,1)S(1)}, bf16[96,3,2560]{2,0,1:T(8,128)(2,1)}, u32[]{:S(2)}) copy-start(bf16[96,3,2560]{2,0,1:T(8,128)(2,1)} %param.7) | copy-start | bytes 4423684
  4.5 16.8 %all-to-all-start = ((bf16[4,768,128]{2,1,0:T(8,128)(2,1)}), bf16[4,768,128]{2,1,0:T(8,128)(2,1)S(1)}, u32[]{:S(2)}, u32[]{:S(2)}) async-start(bf16[4,768,128]{2,1,0:T(8,128)(2,1)} %shard_map.73), calls=%async_computation | async-start | bytes 1572864 | tf_op jit(solution)/shard_map/all_to_all | solution.py:25
  9.0 31.3 %copy-start.3 = (bf16[96,3,768]{2,0,1:T(8,128)(2,1)S(1)}, bf16[96,3,768]{2,0,1:T(8,128)(2,1)}, u32[]{:S(2)}) copy-start(bf16[96,3,768]{2,0,1:T(8,128)(2,1)} %param.8) | copy-start | bytes 1327108
  21.2 12.7 %all-to-all-start.2 = ((bf16[4,576,128]{2,1,0:T(8,128)(2,1)}), bf16[4,576,128]{2,1,0:T(8,128)(2,1)S(1)}, u32[]{:S(2)}, u32[]{:S(2)}) async-start(bf16[4,576,128]{2,1,0:T(8,128)(2,1)} %shard_map.75), calls=%async_computation.2 | async-start | bytes 1179648 | tf_op jit(solution)/shard_map/all_to_all | solution.py:25
  24.7 24.7 %copy-start.5 = (s32[128]{0:T(128)S(1)}, s32[128]{0:T(128)}, u32[]{:S(2)}) copy-start(s32[128]{0:T(128)} %param.11) | copy-start | bytes 1540
  24.7 30.8 %copy-start.4 = (bf16[640,64]{0,1:T(8,128)(2,1)S(1)}, bf16[640,64]{0,1:T(8,128)(2,1)}, u32[]{:S(2)}) copy-start(bf16[640,64]{0,1:T(8,128)(2,1)} %param.9) | copy-start | bytes 245764
  24.7 34.1 %collective-permute-start.1 = (bf16[4,768,128]{2,1,0:T(8,128)(2,1)S(1)}, bf16[4,768,128]{2,1,0:T(8,128)(2,1)}, u32[]{:S(2)}, u32[]{:S(2)}) collective-permute-start(bf16[4,768,128]{2,1,0:T(8,128)(2,1)S(1)} %all-to-all-done.own_ref), channel_id=1, source_target_pairs={{4,0},{8,4},{12,8},{16,12},{20,16},{24,20},{28,24},{32,28},{36,32}... | collective-permute-start | bytes 2359304 | tf_op jit(solution)/shard_map/ppermute | solution.py:21
  29.5 29.4 %collective-permute-start = (bf16[4,768,128]{2,1,0:T(8,128)(2,1)S(1)}, bf16[4,768,128]{2,1,0:T(8,128)(2,1)}, u32[]{:S(2)}, u32[]{:S(2)}) collective-permute-start(bf16[4,768,128]{2,1,0:T(8,128)(2,1)S(1)} %all-to-all-done.own_ref), channel_id=1, source_target_pairs={{0,4},{4,8},{8,12},{12,16},{16,20},{20,24},{24,28},{28,32},{32,36}... | collective-permute-start | bytes 2359304 | tf_op jit(solution)/shard_map/ppermute | solution.py:21
  34.0 21.6 %collective-permute-start.3 = (bf16[4,576,128]{2,1,0:T(8,128)(2,1)S(1)}, bf16[4,576,128]{2,1,0:T(8,128)(2,1)}, u32[]{:S(2)}, u32[]{:S(2)}) collective-permute-start(bf16[4,576,128]{2,1,0:T(8,128)(2,1)S(1)} %all-to-all-done.2.own_ref), channel_id=1, source_target_pairs={{4,0},{8,4},{12,8},{16,12},{20,16},{24,20},{28,24},{32,28},{36,32}... | collective-permute-start | bytes 1769480 | tf_op jit(solution)/shard_map/ppermute | solution.py:21
  38.4 17.1 %collective-permute-start.2 = (bf16[4,576,128]{2,1,0:T(8,128)(2,1)S(1)}, bf16[4,576,128]{2,1,0:T(8,128)(2,1)}, u32[]{:S(2)}, u32[]{:S(2)}) collective-permute-start(bf16[4,576,128]{2,1,0:T(8,128)(2,1)S(1)} %all-to-all-done.2.own_ref), channel_id=1, source_target_pairs={{0,4},{4,8},{8,12},{12,16},{16,20},{20,24},{24,28},{28,32},{32,36}... | collective-permute-start | bytes 1769480 | tf_op jit(solution)/shard_map/ppermute | solution.py:21
  41.8 13.7 %all-to-all-start.1 = ((bf16[4,624,128]{2,1,0:T(8,128)(2,1)}), bf16[4,624,128]{2,1,0:T(8,128)(2,1)S(1)}, u32[]{:S(2)}, u32[]{:S(2)}) async-start(bf16[4,624,128]{2,1,0:T(8,128)(2,1)} %shard_map.74), calls=%async_computation.1 | async-start | bytes 1277952 | tf_op jit(solution)/shard_map/all_to_all | solution.py:25

commit v2 on v0

v2 whole, which is shorter than its diff:
```python
import math

import jax
import jax.numpy as jnp
from jax import lax
from jax.experimental import pallas as pl
from jax.experimental.pallas import tpu as pltpu
from jax.sharding import PartitionSpec as P

HD = 128
TILE = 384
SCALE = math.log2(math.e) / math.sqrt(HD)
LIMIT = 24 * 1024 * 1024
WIDE = 56 * 1024 * 1024
ANY = pl.BlockSpec(memory_space=pl.ANY)
HBM = pl.BlockSpec(memory_space=pltpu.HBM)
VMEM = pl.BlockSpec(memory_space=pltpu.VMEM)
SMEM = pl.BlockSpec(memory_space=pltpu.SMEM)


def traded(block, axis, first):
    lows = range(first, lax.axis_size(axis) - 1, 2)
    return lax.ppermute(block, axis, [p for i in lows for p in ((i, i + 1), (i + 1, i))])


def swapped(block):
    return lax.all_to_all(block, "grp", 0, 0)


def guide_pair(dst):
    return ((0, 1), (2, 1), (3, 4), (5, 4))[dst]


def times(left, right, dims):
    return lax.dot_general(left, right, (dims, ((), ())), preferred_element_type=jnp.float32)


def projected(values, head):
    return times(values, head, ((1,), (1,))).astype(jnp.bfloat16)


def pack(main, guide, guide_head, groups, heads):
    tok = main.shape[1]
    rows = (2 * heads + 3) * tok
    q_rows = (heads + 1) * tok + tok // 2
    half = guide_head.shape[0]

    def kernel(main_ref, guide_ref, heads_ref, out_ref, q_ref, m_buf, g_buf, head_ref, sem):
        order = (1, 2, 0)
        copies = [pltpu.make_async_copy(main_ref.at[i], m_buf.at[i], sem.at[i]) for i in order]
        copies += [pltpu.make_async_copy(guide_ref.at[i], g_buf.at[i], sem.at[3 + i]) for i in order]
        copies.append(pltpu.make_async_copy(heads_ref, head_ref, sem.at[6]))
        for copy in copies:
            copy.start()
        for i, copy in zip(order, copies):
            copy.wait()
            to = (q_ref, out_ref, out_ref)[i]
            for g in range(groups):
                for h in range(heads):
                    at = (h + (heads if i == 2 else 0)) * tok
                    to[g, pl.ds(at, tok), :] = m_buf[i, :, pl.ds((g * heads + h) * HD, HD)]
        for copy in copies[3:]:
            copy.wait()
        for g in range(groups):
            whole, shared = guide_pair(g)
            for i, head in enumerate((whole, shared)):
                cols = pl.ds(head * HD, HD)
                out_ref[g, pl.ds((2 * heads + i) * tok, tok), :] = g_buf[1, :, cols]
                out_ref[g, pl.ds((2 * heads + 2) * tok, tok), pl.ds(i * half, half)] = projected(
                    g_buf[2, :, cols], head_ref[:, cols]
                )
            q_ref[g, pl.ds(heads * tok, tok), :] = g_buf[0, :, pl.ds(whole * HD, HD)]
            q_ref[g, pl.ds((heads + 1) * tok, tok // 2), :] = g_buf[
                0, pl.ds((g % 2) * (tok // 2), tok // 2), pl.ds(shared * HD, HD)
            ]

    return pl.pallas_call(
        kernel,
        out_shape=[
            jax.ShapeDtypeStruct((groups, rows, HD), jnp.bfloat16),
            jax.ShapeDtypeStruct((groups, q_rows, HD), jnp.bfloat16),
        ],
        in_specs=[HBM, HBM, HBM],
        out_specs=[VMEM, VMEM],
        scratch_shapes=[
            pltpu.VMEM(main.shape, jnp.bfloat16),
            pltpu.VMEM(guide.shape, jnp.bfloat16),
            pltpu.VMEM(guide_head.shape, jnp.bfloat16),
            pltpu.SemaphoreType.DMA((7,)),
        ],
        compiler_params=pltpu.CompilerParams(vmem_limit_bytes=WIDE),
    )(main, guide, guide_head)


def project_values(own, main_head, heads, tok):
    groups = own.shape[0]
    half = main_head.shape[0]
    rows = heads * tok + heads * tok // 2 + 3 * tok

    def kernel(own_ref, heads_ref, out_ref, buf, head_ref, sem):
        copies = [
            pltpu.make_async_copy(own_ref, buf, sem.at[0]),
            pltpu.make_async_copy(heads_ref, head_ref, sem.at[1]),
        ]
        for copy in copies:
            copy.start()
        for copy in copies:
            copy.wait()
        out_ref[:, pl.ds(0, heads * tok), :] = buf[:, pl.ds(0, heads * tok), :]
        for h in range(heads):
            values = buf[:, pl.ds((heads + h) * tok, tok), :].reshape(groups * tok, HD)
            moved = projected(values, head_ref[:, pl.ds(h * HD, HD)]).reshape(groups, tok, half)
            at = (heads + h // 2) * tok
            if h == heads - 1 and h % 2 == 0:
                out_ref[:, pl.ds(at, tok // 2), pl.ds(0, half)] = moved[:, : tok // 2]
                out_ref[:, pl.ds(at, tok // 2), pl.ds(half, half)] = moved[:, tok // 2 :]
            else:
                out_ref[:, pl.ds(at, tok), pl.ds((h % 2) * half, half)] = moved
        out_ref[:, pl.ds(rows - 3 * tok, 3 * tok), :] = buf[:, pl.ds(2 * heads * tok, 3 * tok), :]

    return pl.pallas_call(
        kernel,
        out_shape=jax.ShapeDtypeStruct((groups, rows, HD), jnp.bfloat16),
        in_specs=[ANY, HBM],
        out_specs=VMEM,
        scratch_shapes=[
            pltpu.VMEM(own.shape, jnp.bfloat16),
            pltpu.VMEM(main_head.shape, jnp.bfloat16),
            pltpu.SemaphoreType.DMA((2,)),
        ],
        compiler_params=pltpu.CompilerParams(vmem_limit_bytes=LIMIT),
    )(own, main_head)


def attention(window_start, timestep, own, across, beside, queries, heads, tok, half):
    groups, rows, _ = own.shape
    q_rows = queries.shape[1]
    span = groups * tok
    units = [(h * tok, (heads + h // 2) * tok, h % 2, h * tok, tok) for h in range(heads)]
    units += [(rows - (3 - i) * tok, rows - tok, i, (heads + i) * tok, tok // (i + 1)) for i in (0, 1)]

    def kernel(start_ref, step_ref, own_ref, across_ref, beside_ref, q_ref, out_ref,
               kv, s_buf, w_buf, sem):
        tile = lax.axis_index("seq")
        beside = (start_ref[tile] == tile) == (lax.rem(tile, 2) == 0)
        pieces = [(0, heads * tok), (heads * tok, rows - heads * tok)]

        @pl.when(beside)
        def _():
            for i, (at, count) in enumerate(pieces):
                part = pl.ds(at, count)
                pltpu.make_async_copy(beside_ref.at[:, part], kv.at[:, part], sem.at[i]).start()

        @pl.when(jnp.logical_not(beside))
        def _():
            for i, (at, count) in enumerate(pieces):
                part = pl.ds(at, count)
                pltpu.make_async_copy(across_ref.at[:, part], kv.at[:, part], sem.at[i]).start()

        pltpu.make_async_copy(
            across_ref.at[:, pl.ds(*pieces[0])], kv.at[:, pl.ds(*pieces[0])], sem.at[0]
        ).wait()

        def keys(buf, u):
            return buf[:, pl.ds(units[u][0], tok), :].reshape(span, HD)

        def values(buf, u):
            _, at, side, *_ = units[u]
            if u == heads - 1 and u % 2 == 0:
                found = buf[:, pl.ds(at, tok // 2), :]
                found = jnp.concatenate([found[..., :half], found[..., half:]], axis=1)
            else:
                found = buf[:, pl.ds(at, tok), pl.ds(side * half, half)]
            return found.reshape(span, half)

        def score(u):
            _, _, _, at, count = units[u]
            query = q_ref[:, pl.ds(at, count), :].reshape(groups * count, HD)
            for i, buf in enumerate((own_ref, kv)):
                s_buf[u % 2, pl.ds(0, groups * count), pl.ds(i * span, span)] = times(
                    query, keys(buf, u), ((1,), (1,))
                )

        def soften(u):
            for at in range(0, groups * units[u][-1], 96):
                part = pl.ds(at, 96)
                scores = s_buf[u % 2, part, :]
                top = jnp.max(scores, axis=-1, keepdims=True)
                lifted = jnp.exp2((scores - top) * SCALE)
                share = 1.0 / jnp.sum(lifted, axis=-1, keepdims=True)
                w_buf[u % 2, part, :] = (lifted * share).astype(jnp.bfloat16)

        def mix(u):
            part = pl.ds(0, groups * units[u][-1])
            return sum(
                times(w_buf[u % 2, part, pl.ds(i * span, span)], values(buf, u), ((1,), (0,)))
                for i, buf in enumerate((own_ref, kv))
            )

        mixes = []
        score(0)
        for u in range(len(units)):
            if u + 1 < len(units):
                score(u + 1)
            soften(u)
            if u == 0:
                pltpu.make_async_copy(
                    across_ref.at[:, pl.ds(*pieces[1])], kv.at[:, pl.ds(*pieces[1])], sem.at[1]
                ).wait()
            mixes.append(mix(u))
        main = sum(mixes[1:heads], mixes[0])
        whole, shared = mixes[heads:]
        shared = shared.reshape(groups, tok // 2, half)
        blank = jnp.zeros_like(shared)
        upper = lax.rem(lax.axis_index("grp"), 2) != 0
        shared = jnp.concatenate(
            [jnp.where(upper, blank, shared), jnp.where(upper, shared, blank)], axis=1
        )
        w = 1.0 + 2.0 * step_ref[0].astype(jnp.float32) / 999.0
        for j in range(groups):
            part = slice(j * tok, (j + 1) * tok)
            out_ref[j] = (w * main[part] + (1.0 - w) * (whole[part] + shared[j])).T

    flops = int(4 * (heads + 1.5) * groups * tok * 2 * groups * tok * HD)
    return pl.pallas_call(
        kernel,
        out_shape=jax.ShapeDtypeStruct((groups, half, tok), jnp.float32),
        in_specs=[SMEM] * 2 + [VMEM, ANY, ANY, VMEM],
        out_specs=VMEM,
        scratch_shapes=[
            pltpu.VMEM((groups, rows, HD), jnp.bfloat16),
            pltpu.VMEM((2, span, 2 * span), jnp.float32),
            pltpu.VMEM((2, span, 2 * span), jnp.bfloat16),
            pltpu.SemaphoreType.DMA((4,)),
        ],
        compiler_params=pltpu.CompilerParams(vmem_limit_bytes=LIMIT),
        cost_estimate=pl.CostEstimate(flops=flops, bytes_accessed=3 * rows * groups * HD * 2, transcendentals=0),
    )(window_start, timestep, own, across, beside, queries)


def body(main_qkv, guide_qkv, main_head, guide_head, window_start, timestep):
    groups = lax.axis_size("grp")
    tok = main_qkv.shape[0]
    heads = main_head.shape[0] // HD
    half = main_head.shape[1]
    assert groups * tok == TILE and window_start.shape[0] == lax.axis_size("seq")
    main = main_qkv.transpose(1, 0, 2)
    guide = guide_qkv.transpose(1, 0, 2)

    keys, queries = pack(main, guide, guide_head.T, groups, heads)
    gathered = swapped(keys)
    own = project_values(gathered, main_head.T, heads, tok)
    across, beside = traded(own, "seq", 1), traded(own, "seq", 0)
    queries = swapped(queries)
    part = attention(window_start, timestep, own, across, beside, queries, heads, tok, half)
    return jnp.sum(swapped(part), axis=0).T


def solution(mesh):
    in_specs = (
        P(("seq", "grp"), None, None),
        P(("seq", "grp"), None, None),
        P("grp", None),
        P(),
        P(),
        P(),
    )
    out_specs = P(("seq", "grp"), None)
    return jax.shard_map(body, mesh=mesh, in_specs=in_specs, out_specs=out_specs, check_vma=False)
```

time: 172 us -> 61.9 us (0.36)
  the two profiles are of different devices: /device:TPU:6 before, /device:TPU:128 now
where the time goes in v2:
time: 61.9 us; the launch traced here: 61.5 us
  blocking collectives  30.5 us (49%)
  waiting for transfers between devices  10.9 us (18%)
  starting transfers between devices  9.73 us (16%)
  Pallas kernels  9.03 us (15%)
  between operations  0.71 us (1%)
  other arithmetic  0.63 us (1%)
    all_to_all x2, blocking collectives, swapped(): return lax.all_to_all(block, 'grp', 0, 0)  30.5 us
    all_to_all x1, waiting for transfers between devices, swapped(): return lax.all_to_all(block, 'grp', 0, 0)  9.67 us
    ppermute x2, starting transfers between devices, traded(): lax.ppermute(block, axis, [p for i in lows for p in ((i, i + 1), (i + 1,...  6.24 us
    pallas_call x1, Pallas kernels, attention(): pl.pallas_call(kernel, out_shape=jax.ShapeDtypeStruct((groups, half, tok)...  5.07 us
    all_to_all x1, starting transfers between devices, swapped(): return lax.all_to_all(block, 'grp', 0, 0)  3.49 us
    pallas_call x1, Pallas kernels, pack(): pl.pallas_call(kernel, out_shape=[jax.ShapeDtypeStruct((groups, rows, HD)...  3.05 us
  transfers between devices with their start and end apart: 3, of which 2 were waited for; matrix products, arithmetic and copies ran while one was open for 0% of the time, Pallas kernels for 0%

profile of v2, /device:TPU:128, one launch (start us, length us, event | category | flops | bytes accessed | tf_op | source)
XLA Modules:
  0.0 61.5 jit_solution(16127299226582784981)
XLA Ops:
  0.0 3.1 %shard_map.64 = (bf16[4,1248,128]{2,1,0:T(8,128)(2,1)}, bf16[4,624,128]{2,1,0:T(8,128)(2,1)}) custom-call(bf16[3,96,2560]{2,1,0:T(8,128)(2,1)} %bitcast.6, bf16[3,96,768]{2,1,0:T(8,128)(2,1)} %bitcast.7, bf16[64,768]{1,0:T(8,128)(2,1)} %bitcast.8), custom_call_target="tpu_custom_call" | custom-call | tf_op jit(solution)/shard_map/pallas_call | solution.py:77
  3.1 0.0 copy-start
  3.1 22.2 %all_to_all.15.own_ref = bf16[4,1248,128]{2,1,0:T(8,128)(2,1)S(1)} all-to-all(bf16[4,1248,128]{2,1,0:T(8,128)(2,1)} %get-tuple-element.7), channel_id=1, replica_groups=mesh['seq'=128,'grp'=4] {'grp'}, dimensions={0} | all-to-all | bytes 2555904 | tf_op jit(solution)/shard_map/all_to_all | solution.py:27
  25.2 0.0 copy-done
  25.2 0.0 copy-start.1
  25.2 0.9 %shard_map.65.own_ref = bf16[4,1008,128]{2,1,0:T(8,128)(2,1)S(1)} custom-call(bf16[4,1248,128]{2,1,0:T(8,128)(2,1)S(1)} %all_to_all.15.own_ref, bf16[64,640]{1,0:T(8,128)(2,1)S(1)} %bitcast.5), custom_call_target="tpu_custom_call" | custom-call | tf_op jit(solution)/shard_map/pallas_call | solution.py:121
  26.1 1.9 %collective-permute-start.1 = (bf16[4,1008,128]{2,1,0:T(8,128)(2,1)S(1)}, bf16[4,1008,128]{2,1,0:T(8,128)(2,1)S(1)}, u32[]{:S(2)}, u32[]{:S(2)}) collective-permute-start(bf16[4,1008,128]{2,1,0:T(8,128)(2,1)S(1)} %shard_map.65.own_ref), channel_id=1, source_target_pairs={{0,4},{4,0},{8,12},{12,8},{16,20},{20,16},{24,28},{28,24},{32,36},... | collective-permute-start | bytes 3096584 | tf_op jit(solution)/shard_map/ppermute | solution.py:23
  28.1 4.3 %collective-permute-start = (bf16[4,1008,128]{2,1,0:T(8,128)(2,1)S(1)}, bf16[4,1008,128]{2,1,0:T(8,128)(2,1)}, u32[]{:S(2)}, u32[]{:S(2)}) collective-permute-start(bf16[4,1008,128]{2,1,0:T(8,128)(2,1)S(1)} %shard_map.65.own_ref), channel_id=1, source_target_pairs={{4,8},{8,4},{12,16},{16,12},{20,24},{24,20},{28,32},{32,28},{36,40... | collective-permute-start | bytes 3096584 | tf_op jit(solution)/shard_map/ppermute | solution.py:23
  32.4 3.5 %all-to-all-start.1 = ((bf16[4,624,128]{2,1,0:T(8,128)(2,1)}), bf16[4,624,128]{2,1,0:T(8,128)(2,1)S(1)}, u32[]{:S(2)}, u32[]{:S(2)}) async-start(bf16[4,624,128]{2,1,0:T(8,128)(2,1)} %get-tuple-element.8), calls=%async_computation.1 | async-start | bytes 1277952 | tf_op jit(solution)/shard_map/all_to_all | solution.py:27
  36.5 9.7 %all-to-all-done.1.q_ref = bf16[4,624,128]{2,1,0:T(8,128)(2,1)S(1)} async-done(((bf16[4,624,128]{2,1,0:T(8,128)(2,1)}), bf16[4,624,128]{2,1,0:T(8,128)(2,1)S(1)}, u32[]{:S(2)}, u32[]{:S(2)}) %all-to-all-start.1) | async-done | bytes 639008 | tf_op jit(solution)/shard_map/all_to_all | solution.py:27
  46.2 0.0 collective-permute-done.1.beside_ref
  46.2 1.2 %collective-permute-done.across_ref = bf16[4,1008,128]{2,1,0:T(8,128)(2,1)} collective-permute-done((bf16[4,1008,128]{2,1,0:T(8,128)(2,1)S(1)}, bf16[4,1008,128]{2,1,0:T(8,128)(2,1)}, u32[]{:S(2)}, u32[]{:S(2)}) %collective-permute-start) | collective-permute-done | bytes 1032224 | tf_op jit(solution)/shard_map/ppermute | solution.py:23
  47.4 0.0 copy-done.1
  47.4 5.1 %shard_map.66 = f32[4,64,96]{2,1,0:T(8,128)S(1)} custom-call(s32[128]{0:T(128)S(1)} %copy-done.1, s32[1]{0:T(128)S(6)} %copy.7.step_ref, bf16[4,1008,128]{2,1,0:T(8,128)(2,1)S(1)} %shard_map.65.own_ref, bf16[4,1008,128]{2,1,0:T(8,128)(2,1)} %collective-permute-done.across_ref, bf16[4,1008,128]{2,1,0:T(8,128)(2,1)S(1)} %collective-permute-done.1.beside_ref, ...), custom_call_target="tpu_custom_call" | custom-call | flops 981467136 | bytes 3096576 | tf_op jit(solution)/shard_map/pallas_call | solution.py:225
  52.5 8.4 %all_to_all.16 = f32[4,64,96]{2,1,0:T(8,128)S(1)} all-to-all(f32[4,64,96]{2,1,0:T(8,128)S(1)} %shard_map.66), channel_id=1, replica_groups=mesh['seq'=128,'grp'=4] {'grp'}, dimensions={0} | all-to-all | bytes 196608 | tf_op jit(solution)/shard_map/all_to_all | solution.py:27
  60.9 0.6 %reduce_sum.9 = f32[64,96]{1,0:T(8,128)} reduce(f32[4,64,96]{2,1,0:T(8,128)S(1)} %all_to_all.16, f32[]{:T(128)} %constant.0.clone.1), dimensions={0}, to_apply=%region_0.0 | reduce | flops 18432 | bytes 122884 | tf_op jit(solution)/shard_map/reduce_sum | solution.py:256
Async XLA Ops:
  3.1 22.2 %copy-start = (bf16[640,64]{0,1:T(8,128)(2,1)S(1)}, bf16[640,64]{0,1:T(8,128)(2,1)}, u32[]{:S(2)}) copy-start(bf16[640,64]{0,1:T(8,128)(2,1)} %param.8) | copy-start | bytes 245764
  25.2 22.2 %copy-start.1 = (s32[128]{0:T(128)S(1)}, s32[128]{0:T(128)}, u32[]{:S(2)}) copy-start(s32[128]{0:T(128)} %start_ref.1) | copy-start | bytes 1540
  26.1 20.1 %collective-permute-start.1 = (bf16[4,1008,128]{2,1,0:T(8,128)(2,1)S(1)}, bf16[4,1008,128]{2,1,0:T(8,128)(2,1)S(1)}, u32[]{:S(2)}, u32[]{:S(2)}) collective-permute-start(bf16[4,1008,128]{2,1,0:T(8,128)(2,1)S(1)} %shard_map.65.own_ref), channel_id=1, source_target_pairs={{0,4},{4,0},{8,12},{12,8},{16,20},{20,16},{24,28},{28,24},{32,36},... | collective-permute-start | bytes 3096584 | tf_op jit(solution)/shard_map/ppermute | solution.py:23
  28.1 19.4 %collective-permute-start = (bf16[4,1008,128]{2,1,0:T(8,128)(2,1)S(1)}, bf16[4,1008,128]{2,1,0:T(8,128)(2,1)}, u32[]{:S(2)}, u32[]{:S(2)}) collective-permute-start(bf16[4,1008,128]{2,1,0:T(8,128)(2,1)S(1)} %shard_map.65.own_ref), channel_id=1, source_target_pairs={{4,8},{8,4},{12,16},{16,12},{20,24},{24,20},{28,32},{32,28},{36,40... | collective-permute-start | bytes 3096584 | tf_op jit(solution)/shard_map/ppermute | solution.py:23
  32.4 13.8 %all-to-all-start.1 = ((bf16[4,624,128]{2,1,0:T(8,128)(2,1)}), bf16[4,624,128]{2,1,0:T(8,128)(2,1)S(1)}, u32[]{:S(2)}, u32[]{:S(2)}) async-start(bf16[4,624,128]{2,1,0:T(8,128)(2,1)} %get-tuple-element.8), calls=%async_computation.1 | async-start | bytes 1277952 | tf_op jit(solution)/shard_map/all_to_all | solution.py:27

commit v3 on v2

v3 whole, which is shorter than its diff:
```python
import math

import jax
import jax.numpy as jnp
from jax import lax
from jax.experimental import pallas as pl
from jax.experimental.pallas import tpu as pltpu
from jax.sharding import PartitionSpec as P

HD = 128
TILE = 384
SCALE = math.log2(math.e) / math.sqrt(HD)
LIMIT = 16 * 1024 * 1024
WIDE = 56 * 1024 * 1024
ANY = pl.BlockSpec(memory_space=pl.ANY)
HBM = pl.BlockSpec(memory_space=pltpu.HBM)
VMEM = pl.BlockSpec(memory_space=pltpu.VMEM)
SMEM = pl.BlockSpec(memory_space=pltpu.SMEM)


def traded(block, axis, first):
    lows = range(first, lax.axis_size(axis) - 1, 2)
    return lax.ppermute(block, axis, [p for i in lows for p in ((i, i + 1), (i + 1, i))])


def swapped(block):
    return lax.all_to_all(block, "grp", 0, 0)


def guide_pair(dst):
    return ((0, 1), (2, 1), (3, 4), (5, 4))[dst]


def times(left, right, dims):
    return lax.dot_general(left, right, (dims, ((), ())), preferred_element_type=jnp.float32)


def projected(values, head):
    return times(values, head, ((1,), (1,))).astype(jnp.bfloat16)


def spread(source, target, first, groups, heads):
    tok = source.shape[0]
    for g in range(groups):
        for h in range(heads):
            target[g, pl.ds(first + h * tok, tok), :] = source[:, pl.ds((g * heads + h) * HD, HD)]


def pack_keys(main, guide, guide_head, groups, heads):
    tok = main.shape[1]
    rows = (2 * heads + 3) * tok
    half = guide_head.shape[0]

    def kernel(main_ref, guide_ref, heads_ref, out_ref, m_buf, g_buf, head_ref, buf, sem, out_sem):
        main_in = [pltpu.make_async_copy(main_ref.at[1 + i], m_buf.at[i], sem.at[i]) for i in (0, 1)]
        guide_in = [
            pltpu.make_async_copy(heads_ref, head_ref, sem.at[2]),
            pltpu.make_async_copy(guide_ref.at[pl.ds(1, 2)], g_buf, sem.at[3]),
        ]
        for copy in guide_in + main_in:
            copy.start()
        copies = []

        def put(first, count):
            part = pl.ds(first, count)
            copies.append(
                pltpu.make_async_copy(buf.at[:, part], out_ref.at[:, part], out_sem.at[len(copies)])
            )
            copies[-1].start()

        def guides():
            for copy in guide_in:
                copy.wait()
            for g in range(groups):
                for i, head in enumerate(guide_pair(g)):
                    cols = pl.ds(head * HD, HD)
                    buf[g, pl.ds((2 * heads + i) * tok, tok), :] = g_buf[0, :, cols]
                    buf[g, pl.ds((2 * heads + 2) * tok, tok), pl.ds(i * half, half)] = projected(
                        g_buf[1, :, cols], head_ref[:, cols]
                    )
            put(2 * heads * tok, 3 * tok)

        guides()
        for i, copy in enumerate(main_in):
            copy.wait()
            spread(m_buf.at[i], buf, i * heads * tok, groups, heads)
            put(i * heads * tok, heads * tok)
        for copy in copies:
            copy.wait()

    return pl.pallas_call(
        kernel,
        out_shape=jax.ShapeDtypeStruct((groups, rows, HD), jnp.bfloat16),
        in_specs=[HBM, HBM, HBM],
        out_specs=HBM,
        scratch_shapes=[
            pltpu.VMEM((2,) + main.shape[1:], jnp.bfloat16),
            pltpu.VMEM((2,) + guide.shape[1:], jnp.bfloat16),
            pltpu.VMEM(guide_head.shape, jnp.bfloat16),
            pltpu.VMEM((groups, rows, HD), jnp.bfloat16),
            pltpu.SemaphoreType.DMA((4,)),
            pltpu.SemaphoreType.DMA((3,)),
        ],
        compiler_params=pltpu.CompilerParams(vmem_limit_bytes=WIDE),
    )(main, guide, guide_head)


def pack_queries(main, guide, groups, heads):
    tok = main.shape[1]
    rows = (heads + 1) * tok + tok // 2

    def kernel(main_ref, guide_ref, out_ref, m_buf, g_buf, sem):
        copies = [
            pltpu.make_async_copy(main_ref.at[0], m_buf, sem.at[0]),
            pltpu.make_async_copy(guide_ref.at[0], g_buf, sem.at[1]),
        ]
        for copy in copies:
            copy.start()
        copies[0].wait()
        spread(m_buf, out_ref, 0, groups, heads)
        copies[1].wait()
        for g in range(groups):
            whole, shared = guide_pair(g)
            out_ref[g, pl.ds(heads * tok, tok), :] = g_buf[:, pl.ds(whole * HD, HD)]
            out_ref[g, pl.ds((heads + 1) * tok, tok // 2), :] = g_buf[
                pl.ds((g % 2) * (tok // 2), tok // 2), pl.ds(shared * HD, HD)
            ]

    return pl.pallas_call(
        kernel,
        out_shape=jax.ShapeDtypeStruct((groups, rows, HD), jnp.bfloat16),
        in_specs=[HBM, HBM],
        out_specs=VMEM,
        scratch_shapes=[
            pltpu.VMEM(main.shape[1:], jnp.bfloat16),
            pltpu.VMEM(guide.shape[1:], jnp.bfloat16),
            pltpu.SemaphoreType.DMA((2,)),
        ],
        compiler_params=pltpu.CompilerParams(vmem_limit_bytes=WIDE),
    )(main, guide)


def project_values(own, main_head, heads, tok, after):
    groups = own.shape[0]
    half = main_head.shape[0]
    rows = heads * tok + heads * tok // 2 + 3 * tok

    def kernel(own_ref, head_ref, after_ref, out_ref):
        out_ref[:, pl.ds(0, heads * tok), :] = own_ref[:, pl.ds(0, heads * tok), :]
        for h in range(heads):
            values = own_ref[:, pl.ds((heads + h) * tok, tok), :].reshape(groups * tok, HD)
            moved = projected(values, head_ref[:, pl.ds(h * HD, HD)]).reshape(groups, tok, half)
            at = (heads + h // 2) * tok
            if h == heads - 1 and h % 2 == 0:
                out_ref[:, pl.ds(at, tok // 2), pl.ds(0, half)] = moved[:, : tok // 2]
                out_ref[:, pl.ds(at, tok // 2), pl.ds(half, half)] = moved[:, tok // 2 :]
            else:
                out_ref[:, pl.ds(at, tok), pl.ds((h % 2) * half, half)] = moved
        out_ref[:, pl.ds(rows - 3 * tok, 3 * tok), :] = own_ref[:, pl.ds(2 * heads * tok, 3 * tok), :]

    return pl.pallas_call(
        kernel,
        out_shape=jax.ShapeDtypeStruct((groups, rows, HD), jnp.bfloat16),
        in_specs=[VMEM, VMEM, ANY],
        out_specs=VMEM,
        compiler_params=pltpu.CompilerParams(vmem_limit_bytes=LIMIT),
    )(own, main_head, after)


def cut(block, bounds):
    groups = block.shape[0]
    counts = [b - a for a, b in zip(bounds, bounds[1:])]

    def kernel(ref, *refs):
        outs, sem = refs[:-1], refs[-1]
        copies = [
            pltpu.make_async_copy(ref.at[:, pl.ds(a, count)], out, sem.at[i])
            for i, (a, count, out) in enumerate(zip(bounds, counts, outs))
        ]
        for copy in copies:
            copy.start()
        for copy in copies:
            copy.wait()

    return pl.pallas_call(
        kernel,
        out_shape=[jax.ShapeDtypeStruct((groups, count, HD), jnp.bfloat16) for count in counts],
        in_specs=[ANY],
        out_specs=[ANY] * len(counts),
        scratch_shapes=[pltpu.SemaphoreType.DMA((len(counts),))],
        compiler_params=pltpu.CompilerParams(vmem_limit_bytes=LIMIT),
    )(block)


def attention(window_start, timestep, own, across, beside, queries, heads, tok, half):
    groups, rows, _ = own.shape
    span = groups * tok
    units = [(h * tok, (heads + h // 2) * tok, h % 2, h * tok, tok) for h in range(heads)]
    units += [(rows - (3 - i) * tok, rows - tok, i, (heads + i) * tok, tok // (i + 1)) for i in (0, 1)]

    def kernel(start_ref, step_ref, own_ref, across_ref, *refs):
        beside_refs, (q_ref, out_ref, s_buf, w_buf) = refs[: len(beside)], refs[len(beside) :]
        tile = lax.axis_index("seq")

        def block(parts, at, count):
            for part in parts:
                if at < part.shape[1]:
                    return part[:, pl.ds(at, count), :]
                at -= part.shape[1]

        def keys(parts, u):
            return block(parts, units[u][0], tok).reshape(span, HD)

        def values(parts, u):
            _, at, side, *_ = units[u]
            if u == heads - 1 and u % 2 == 0:
                found = block(parts, at, tok // 2)
                found = jnp.concatenate([found[..., :half], found[..., half:]], axis=1)
            else:
                found = block(parts, at, tok)[..., side * half : (side + 1) * half]
            return found.reshape(span, half)

        def attend(sources):
            def score(u):
                _, _, _, at, count = units[u]
                query = q_ref[:, pl.ds(at, count), :].reshape(groups * count, HD)
                for i, parts in enumerate(sources):
                    s_buf[u % 2, pl.ds(0, groups * count), pl.ds(i * span, span)] = times(
                        query, keys(parts, u), ((1,), (1,))
                    )

            def soften(u):
                for at in range(0, groups * units[u][-1], tok):
                    part = pl.ds(at, tok)
                    scores = s_buf[u % 2, part, :]
                    top = jnp.max(scores, axis=-1, keepdims=True)
                    lifted = jnp.exp2((scores - top) * SCALE)
                    share = 1.0 / jnp.sum(lifted, axis=-1, keepdims=True)
                    w_buf[u % 2, part, :] = (lifted * share).astype(jnp.bfloat16)

            def mix(u):
                part = pl.ds(0, groups * units[u][-1])
                both = jnp.concatenate([values(parts, u) for parts in sources], axis=0)
                return times(w_buf[u % 2, part, :], both, ((1,), (0,)))

            mixes = []
            score(0)
            for u in range(len(units)):
                if u + 1 < len(units):
                    score(u + 1)
                soften(u)
                mixes.append(mix(u))
            main = sum(mixes[1:heads], mixes[0])
            whole, shared = mixes[heads:]
            shared = shared.reshape(groups, tok // 2, half)
            blank = jnp.zeros_like(shared)
            upper = lax.rem(lax.axis_index("grp"), 2) != 0
            shared = jnp.concatenate(
                [jnp.where(upper, blank, shared), jnp.where(upper, shared, blank)], axis=1
            )
            w = 1.0 + 2.0 * step_ref[0].astype(jnp.float32) / 999.0
            for j in range(groups):
                part = slice(j * tok, (j + 1) * tok)
                out_ref[j] = (w * main[part] + (1.0 - w) * (whole[part] + shared[j])).T

        use_beside = (start_ref[tile] == tile) == (lax.rem(tile, 2) == 0)

        @pl.when(use_beside)
        def _():
            attend(([own_ref], beside_refs))

        @pl.when(jnp.logical_not(use_beside))
        def _():
            attend(([own_ref], [across_ref]))

    flops = int(4 * (heads + 1.5) * groups * tok * 2 * groups * tok * HD)
    return pl.pallas_call(
        kernel,
        out_shape=jax.ShapeDtypeStruct((groups, half, tok), jnp.float32),
        in_specs=[SMEM] * 2 + [VMEM] * (3 + len(beside)),
        out_specs=VMEM,
        scratch_shapes=[
            pltpu.VMEM((2, span, 2 * span), jnp.float32),
            pltpu.VMEM((2, span, 2 * span), jnp.bfloat16),
        ],
        compiler_params=pltpu.CompilerParams(vmem_limit_bytes=LIMIT),
        cost_estimate=pl.CostEstimate(flops=flops, bytes_accessed=3 * rows * groups * HD * 2, transcendentals=0),
    )(window_start, timestep, own, across, *beside, queries)


def body(main_qkv, guide_qkv, main_head, guide_head, window_start, timestep):
    groups = lax.axis_size("grp")
    tok = main_qkv.shape[0]
    heads = main_head.shape[0] // HD
    half = main_head.shape[1]
    assert groups * tok == TILE and window_start.shape[0] == lax.axis_size("seq")
    main = main_qkv.transpose(1, 0, 2)
    guide = guide_qkv.transpose(1, 0, 2)

    packed = pack_queries(main, guide, groups, heads)
    gathered = swapped(pack_keys(main, guide, guide_head.T, groups, heads))
    own = project_values(gathered, main_head.T, heads, tok, packed)
    across = traded(own, "seq", 1)
    beside = [traded(part, "seq", 0) for part in cut(own, (0, 3 * tok, 6 * tok, own.shape[1]))]
    queries = swapped(packed)
    part = attention(window_start, timestep, own, across, beside, queries, heads, tok, half)
    return jnp.sum(swapped(part), axis=0).T


def solution(mesh):
    in_specs = (
        P(("seq", "grp"), None, None),
        P(("seq", "grp"), None, None),
        P("grp", None),
        P(),
        P(),
        P(),
    )
    out_specs = P(("seq", "grp"), None)
    return jax.shard_map(body, mesh=mesh, in_specs=in_specs, out_specs=out_specs, check_vma=False)
```

time: 61.9 us -> 58.1 us (0.939)
  the two profiles are of different devices: /device:TPU:128 before, /device:TPU:384 now
where the time goes in v3:
time: 58.1 us; the launch traced here: 57.7 us
  starting transfers between devices  18.8 us (32%)
  waiting for transfers between devices  18.8 us (32%)
  Pallas kernels  10.2 us (18%)
  blocking collectives  8.56 us (15%)
  between operations  0.74 us (1%)
  other arithmetic  0.63 us (1%)
    all_to_all x2, waiting for transfers between devices, swapped(): return lax.all_to_all(block, 'grp', 0, 0)  17.6 us
    ppermute x4, starting transfers between devices, traded(): lax.ppermute(block, axis, [p for i in lows for p in ((i, i + 1), (i + 1,...  10.8 us
    all_to_all x1, blocking collectives, swapped(): return lax.all_to_all(block, 'grp', 0, 0)  8.56 us
    all_to_all x2, starting transfers between devices, swapped(): return lax.all_to_all(block, 'grp', 0, 0)  7.97 us
    pallas_call x1, Pallas kernels, attention(): pl.pallas_call(kernel, out_shape=jax.ShapeDtypeStruct((groups, half, tok)...  4.32 us
    pallas_call x1, Pallas kernels, pack_keys(): pl.pallas_call(kernel, out_shape=jax.ShapeDtypeStruct((groups, rows, HD),...  2.43 us
    pallas_call x1, Pallas kernels, pack_queries(): pl.pallas_call(kernel, out_shape=jax.ShapeDtypeStruct((groups, rows, HD),...  2.02 us
  transfers between devices with their start and end apart: 6, of which 3 were waited for; matrix products, arithmetic and copies ran while one was open for 0% of the time, Pallas kernels for 5%

profile of v3, /device:TPU:384, one launch (start us, length us, event | category | flops | bytes accessed | tf_op | source)
XLA Modules:
  0.0 57.7 jit_solution(4240473741891188817)
XLA Ops:
  0.0 2.4 %shard_map.64 = bf16[4,1248,128]{2,1,0:T(8,128)(2,1)} custom-call(bf16[3,96,2560]{2,1,0:T(8,128)(2,1)} %bitcast.6, bf16[3,96,768]{2,1,0:T(8,128)(2,1)} %bitcast.8, bf16[64,768]{1,0:T(8,128)(2,1)} %bitcast.10), custom_call_target="tpu_custom_call" | custom-call | tf_op jit(solution)/shard_map/pallas_call | solution.py:91
  2.4 4.5 %all-to-all-start = ((bf16[4,1248,128]{2,1,0:T(8,128)(2,1)}), bf16[4,1248,128]{2,1,0:T(8,128)(2,1)S(1)}, u32[]{:S(2)}, u32[]{:S(2)}) async-start(bf16[4,1248,128]{2,1,0:T(8,128)(2,1)} %shard_map.64), calls=%async_computation | async-start | bytes 2555904 | tf_op jit(solution)/shard_map/all_to_all | solution.py:27
  6.9 0.0 copy-start
  6.9 2.0 %shard_map.65.after_ref = bf16[4,624,128]{2,1,0:T(8,128)(2,1)} custom-call(bf16[3,96,2560]{2,1,0:T(8,128)(2,1)} %bitcast.7, bf16[3,96,768]{2,1,0:T(8,128)(2,1)} %bitcast.9), custom_call_target="tpu_custom_call" | custom-call | tf_op jit(solution)/shard_map/pallas_call | solution.py:129
  9.0 15.5 %all-to-all-done.own_ref = bf16[4,1248,128]{2,1,0:T(8,128)(2,1)S(1)} async-done(((bf16[4,1248,128]{2,1,0:T(8,128)(2,1)}), bf16[4,1248,128]{2,1,0:T(8,128)(2,1)S(1)}, u32[]{:S(2)}, u32[]{:S(2)}) %all-to-all-start) | async-done | bytes 1277984 | tf_op jit(solution)/shard_map/all_to_all | solution.py:27
  24.5 0.0 copy-done
  24.5 0.4 shard_map.66.ref.own_ref
  24.9 0.0 copy-start.1
  24.9 4.6 %collective-permute-start = (bf16[4,1008,128]{2,1,0:T(8,128)(2,1)S(1)}, bf16[4,1008,128]{2,1,0:T(8,128)(2,1)S(1)}, u32[]{:S(2)}, u32[]{:S(2)}) collective-permute-start(bf16[4,1008,128]{2,1,0:T(8,128)(2,1)S(1)} %shard_map.66.ref.own_ref), channel_id=1, source_target_pairs={{4,8},{8,4},{12,16},{16,12},{20,24},{24,20},{28,32},{32,28},{36,40... | collective-permute-start | bytes 3096584 | tf_op jit(solution)/shard_map/ppermute | solution.py:23
  29.5 3.5 %all-to-all-start.1 = ((bf16[4,624,128]{2,1,0:T(8,128)(2,1)}), bf16[4,624,128]{2,1,0:T(8,128)(2,1)S(1)}, u32[]{:S(2)}, u32[]{:S(2)}) async-start(bf16[4,624,128]{2,1,0:T(8,128)(2,1)} %shard_map.65.after_ref), calls=%async_computation.1 | async-start | bytes 1277952 | tf_op jit(solution)/shard_map/all_to_all | solution.py:27
  33.0 1.0 %shard_map.67 = (bf16[4,288,128]{2,1,0:T(8,128)(2,1)}, bf16[4,288,128]{2,1,0:T(8,128)(2,1)}, bf16[4,432,128]{2,1,0:T(8,128)(2,1)}) custom-call(bf16[4,1008,128]{2,1,0:T(8,128)(2,1)S(1)} %shard_map.66.ref.own_ref), custom_call_target="tpu_custom_call" | custom-call | tf_op jit(solution)/shard_map/pallas_call | solution.py:185
  34.0 1.9 %collective-permute-start.3 = (bf16[4,432,128]{2,1,0:T(8,128)(2,1)}, bf16[4,432,128]{2,1,0:T(8,128)(2,1)S(1)}, u32[]{:S(2)}, u32[]{:S(2)}) collective-permute-start(bf16[4,432,128]{2,1,0:T(8,128)(2,1)} %get-tuple-element.10), channel_id=1, source_target_pairs={{0,4},{4,0},{8,12},{12,8},{16,20},{20,16},{24,28},{28,24},{32,36},... | collective-permute-start | bytes 1327112 | tf_op jit(solution)/shard_map/ppermute | solution.py:23
  35.9 2.4 %collective-permute-start.1 = (bf16[4,288,128]{2,1,0:T(8,128)(2,1)}, bf16[4,288,128]{2,1,0:T(8,128)(2,1)S(1)}, u32[]{:S(2)}, u32[]{:S(2)}) collective-permute-start(bf16[4,288,128]{2,1,0:T(8,128)(2,1)} %get-tuple-element.8), channel_id=1, source_target_pairs={{0,4},{4,0},{8,12},{12,8},{16,20},{20,16},{24,28},{28,24},{32,36},... | collective-permute-start | bytes 884744 | tf_op jit(solution)/shard_map/ppermute | solution.py:23
  38.3 1.9 %collective-permute-start.2 = (bf16[4,288,128]{2,1,0:T(8,128)(2,1)}, bf16[4,288,128]{2,1,0:T(8,128)(2,1)}, u32[]{:S(2)}, u32[]{:S(2)}) collective-permute-start(bf16[4,288,128]{2,1,0:T(8,128)(2,1)} %get-tuple-element.9), channel_id=1, source_target_pairs={{0,4},{4,0},{8,12},{12,8},{16,20},{20,16},{24,28},{28,24},{32,36},... | collective-permute-start | bytes 884744 | tf_op jit(solution)/shard_map/ppermute | solution.py:23
  40.9 2.1 %all-to-all-done.1.refs_3_ = bf16[4,624,128]{2,1,0:T(8,128)(2,1)S(1)} async-done(((bf16[4,624,128]{2,1,0:T(8,128)(2,1)}), bf16[4,624,128]{2,1,0:T(8,128)(2,1)S(1)}, u32[]{:S(2)}, u32[]{:S(2)}) %all-to-all-start.1) | async-done | bytes 639008 | tf_op jit(solution)/shard_map/all_to_all | solution.py:27
  43.0 0.0 collective-permute-done.1.refs_0_
  43.0 0.0 collective-permute-done.2.refs_1_
  43.0 0.0 collective-permute-done.3.refs_2_
  43.0 1.1 %collective-permute-done.across_ref = bf16[4,1008,128]{2,1,0:T(8,128)(2,1)S(1)} collective-permute-done((bf16[4,1008,128]{2,1,0:T(8,128)(2,1)S(1)}, bf16[4,1008,128]{2,1,0:T(8,128)(2,1)S(1)}, u32[]{:S(2)}, u32[]{:S(2)}) %collective-permute-start) | collective-permute-done | bytes 1032224 | tf_op jit(solution)/shard_map/ppermute | solution.py:23
  44.2 0.0 copy-done.1
  44.2 4.3 %shard_map.68 = f32[4,64,96]{2,1,0:T(8,128)S(1)} custom-call(s32[128]{0:T(128)S(1)} %copy-done.1, s32[1]{0:T(128)S(6)} %copy.7.step_ref, bf16[4,1008,128]{2,1,0:T(8,128)(2,1)S(1)} %shard_map.66.ref.own_ref, bf16[4,1008,128]{2,1,0:T(8,128)(2,1)S(1)} %collective-permute-done.across_ref, bf16[4,288,128]{2,1,0:T(8,128)(2,1)S(1)} %collective-permute-done.1.refs_0_, ...), custom_call_target="tpu_custom_call" | custom-call | flops 981467136 | bytes 3096576 | tf_op jit(solution)/shard_map/pallas_call | solution.py:277
  48.5 8.6 %all_to_all.15 = f32[4,64,96]{2,1,0:T(8,128)S(1)} all-to-all(f32[4,64,96]{2,1,0:T(8,128)S(1)} %shard_map.68), channel_id=1, replica_groups=mesh['seq'=128,'grp'=4] {'grp'}, dimensions={0} | all-to-all | bytes 196608 | tf_op jit(solution)/shard_map/all_to_all | solution.py:27
  57.0 0.6 %reduce_sum.9 = f32[64,96]{1,0:T(8,128)} reduce(f32[4,64,96]{2,1,0:T(8,128)S(1)} %all_to_all.15, f32[]{:T(128)} %constant.0.clone.1), dimensions={0}, to_apply=%region_0.0 | reduce | flops 18432 | bytes 122884 | tf_op jit(solution)/shard_map/reduce_sum | solution.py:307
Async XLA Ops:
  2.4 22.0 %all-to-all-start = ((bf16[4,1248,128]{2,1,0:T(8,128)(2,1)}), bf16[4,1248,128]{2,1,0:T(8,128)(2,1)S(1)}, u32[]{:S(2)}, u32[]{:S(2)}) async-start(bf16[4,1248,128]{2,1,0:T(8,128)(2,1)} %shard_map.64), calls=%async_computation | async-start | bytes 2555904 | tf_op jit(solution)/shard_map/all_to_all | solution.py:27
  6.9 17.6 %copy-start = (bf16[640,64]{0,1:T(8,128)(2,1)S(1)}, bf16[640,64]{0,1:T(8,128)(2,1)}, u32[]{:S(2)}) copy-start(bf16[640,64]{0,1:T(8,128)(2,1)} %param.8) | copy-start | bytes 245764
  24.9 19.3 %copy-start.1 = (s32[128]{0:T(128)S(1)}, s32[128]{0:T(128)}, u32[]{:S(2)}) copy-start(s32[128]{0:T(128)} %start_ref.1) | copy-start | bytes 1540
  24.9 19.3 %collective-permute-start = (bf16[4,1008,128]{2,1,0:T(8,128)(2,1)S(1)}, bf16[4,1008,128]{2,1,0:T(8,128)(2,1)S(1)}, u32[]{:S(2)}, u32[]{:S(2)}) collective-permute-start(bf16[4,1008,128]{2,1,0:T(8,128)(2,1)S(1)} %shard_map.66.ref.own_ref), channel_id=1, source_target_pairs={{4,8},{8,4},{12,16},{16,12},{20,24},{24,20},{28,32},{32,28},{36,40... | collective-permute-start | bytes 3096584 | tf_op jit(solution)/shard_map/ppermute | solution.py:23
  29.5 13.6 %all-to-all-start.1 = ((bf16[4,624,128]{2,1,0:T(8,128)(2,1)}), bf16[4,624,128]{2,1,0:T(8,128)(2,1)S(1)}, u32[]{:S(2)}, u32[]{:S(2)}) async-start(bf16[4,624,128]{2,1,0:T(8,128)(2,1)} %shard_map.65.after_ref), calls=%async_computation.1 | async-start | bytes 1277952 | tf_op jit(solution)/shard_map/all_to_all | solution.py:27
  34.0 9.0 %collective-permute-start.3 = (bf16[4,432,128]{2,1,0:T(8,128)(2,1)}, bf16[4,432,128]{2,1,0:T(8,128)(2,1)S(1)}, u32[]{:S(2)}, u32[]{:S(2)}) collective-permute-start(bf16[4,432,128]{2,1,0:T(8,128)(2,1)} %get-tuple-element.10), channel_id=1, source_target_pairs={{0,4},{4,0},{8,12},{12,8},{16,20},{20,16},{24,28},{28,24},{32,36},... | collective-permute-start | bytes 1327112 | tf_op jit(solution)/shard_map/ppermute | solution.py:23
  35.9 7.1 %collective-permute-start.1 = (bf16[4,288,128]{2,1,0:T(8,128)(2,1)}, bf16[4,288,128]{2,1,0:T(8,128)(2,1)S(1)}, u32[]{:S(2)}, u32[]{:S(2)}) collective-permute-start(bf16[4,288,128]{2,1,0:T(8,128)(2,1)} %get-tuple-element.8), channel_id=1, source_target_pairs={{0,4},{4,0},{8,12},{12,8},{16,20},{20,16},{24,28},{28,24},{32,36},... | collective-permute-start | bytes 884744 | tf_op jit(solution)/shard_map/ppermute | solution.py:23
  38.3 4.7 %collective-permute-start.2 = (bf16[4,288,128]{2,1,0:T(8,128)(2,1)}, bf16[4,288,128]{2,1,0:T(8,128)(2,1)}, u32[]{:S(2)}, u32[]{:S(2)}) collective-permute-start(bf16[4,288,128]{2,1,0:T(8,128)(2,1)} %get-tuple-element.9), channel_id=1, source_target_pairs={{0,4},{4,0},{8,12},{12,8},{16,20},{20,16},{24,28},{28,24},{32,36},... | collective-permute-start | bytes 884744 | tf_op jit(solution)/shard_map/ppermute | solution.py:23

commit v4 on v3

--- a/solution.py
+++ b/solution.py
@@ -230,8 +230,8 @@
                     )
 
             def soften(u):
-                for at in range(0, groups * units[u][-1], tok):
-                    part = pl.ds(at, tok)
+                for at in range(0, groups * units[u][-1], 2 * tok):
+                    part = pl.ds(at, 2 * tok)
                     scores = s_buf[u % 2, part, :]
                     top = jnp.max(scores, axis=-1, keepdims=True)
                     lifted = jnp.exp2((scores - top) * SCALE)
@@ -248,8 +248,10 @@
             for u in range(len(units)):
                 if u + 1 < len(units):
                     score(u + 1)
+                if u:
+                    mixes.append(mix(u - 1))
                 soften(u)
-                mixes.append(mix(u))
+            mixes.append(mix(len(units) - 1))
             main = sum(mixes[1:heads], mixes[0])
             whole, shared = mixes[heads:]
             shared = shared.reshape(groups, tok // 2, half)
@@ -301,7 +303,7 @@
     gathered = swapped(pack_keys(main, guide, guide_head.T, groups, heads))
     own = project_values(gathered, main_head.T, heads, tok, packed)
     across = traded(own, "seq", 1)
-    beside = [traded(part, "seq", 0) for part in cut(own, (0, 3 * tok, 6 * tok, own.shape[1]))]
+    beside = [traded(part, "seq", 0) for part in cut(own, (0, 4 * tok, own.shape[1] - 2 * tok, own.shape[1]))]
     queries = swapped(packed)
     part = attention(window_start, timestep, own, across, beside, queries, heads, tok, half)
     return jnp.sum(swapped(part), axis=0).T

time: 58.1 us -> 57.7 us (level)
  no operation moved by 1% of the time
where the time goes in v4:
time: 57.7 us; the launch traced here: 57.3 us
  starting transfers between devices  18.8 us (33%)
  waiting for transfers between devices  18.7 us (32%)
  Pallas kernels  9.99 us (17%)
  blocking collectives  8.41 us (15%)
  between operations  0.74 us (1%)
  other arithmetic  0.63 us (1%)
    all_to_all x2, waiting for transfers between devices, swapped(): return lax.all_to_all(block, 'grp', 0, 0)  17.6 us
    ppermute x4, starting transfers between devices, traded(): lax.ppermute(block, axis, [p for i in lows for p in ((i, i + 1), (i + 1,...  10.8 us
    all_to_all x1, blocking collectives, swapped(): return lax.all_to_all(block, 'grp', 0, 0)  8.41 us
    all_to_all x2, starting transfers between devices, swapped(): return lax.all_to_all(block, 'grp', 0, 0)  7.97 us
    pallas_call x1, Pallas kernels, attention(): pl.pallas_call(kernel, out_shape=jax.ShapeDtypeStruct((groups, half, tok)...  4.13 us
    pallas_call x1, Pallas kernels, pack_keys(): pl.pallas_call(kernel, out_shape=jax.ShapeDtypeStruct((groups, rows, HD),...  2.42 us
    pallas_call x1, Pallas kernels, pack_queries(): pl.pallas_call(kernel, out_shape=jax.ShapeDtypeStruct((groups, rows, HD),...  2.05 us
  transfers between devices with their start and end apart: 6, of which 3 were waited for; matrix products, arithmetic and copies ran while one was open for 0% of the time, Pallas kernels for 5%

profile of v4, /device:TPU:384, one launch (start us, length us, event | category | flops | bytes accessed | tf_op | source)
XLA Modules:
  0.0 57.3 jit_solution(15553984954934730403)
XLA Ops:
  0.0 2.4 %shard_map.64 = bf16[4,1248,128]{2,1,0:T(8,128)(2,1)} custom-call(bf16[3,96,2560]{2,1,0:T(8,128)(2,1)} %bitcast.6, bf16[3,96,768]{2,1,0:T(8,128)(2,1)} %bitcast.8, bf16[64,768]{1,0:T(8,128)(2,1)} %bitcast.10), custom_call_target="tpu_custom_call" | custom-call | tf_op jit(solution)/shard_map/pallas_call | solution.py:91
  2.4 4.5 %all-to-all-start = ((bf16[4,1248,128]{2,1,0:T(8,128)(2,1)}), bf16[4,1248,128]{2,1,0:T(8,128)(2,1)S(1)}, u32[]{:S(2)}, u32[]{:S(2)}) async-start(bf16[4,1248,128]{2,1,0:T(8,128)(2,1)} %shard_map.64), calls=%async_computation | async-start | bytes 2555904 | tf_op jit(solution)/shard_map/all_to_all | solution.py:27
  6.9 0.0 copy-start
  6.9 2.0 %shard_map.65.after_ref = bf16[4,624,128]{2,1,0:T(8,128)(2,1)} custom-call(bf16[3,96,2560]{2,1,0:T(8,128)(2,1)} %bitcast.7, bf16[3,96,768]{2,1,0:T(8,128)(2,1)} %bitcast.9), custom_call_target="tpu_custom_call" | custom-call | tf_op jit(solution)/shard_map/pallas_call | solution.py:129
  9.0 15.5 %all-to-all-done.own_ref = bf16[4,1248,128]{2,1,0:T(8,128)(2,1)S(1)} async-done(((bf16[4,1248,128]{2,1,0:T(8,128)(2,1)}), bf16[4,1248,128]{2,1,0:T(8,128)(2,1)S(1)}, u32[]{:S(2)}, u32[]{:S(2)}) %all-to-all-start) | async-done | bytes 1277984 | tf_op jit(solution)/shard_map/all_to_all | solution.py:27
  24.5 0.0 copy-done
  24.5 0.4 shard_map.66.ref.own_ref
  24.9 0.0 copy-start.1
  24.9 4.6 %collective-permute-start = (bf16[4,1008,128]{2,1,0:T(8,128)(2,1)S(1)}, bf16[4,1008,128]{2,1,0:T(8,128)(2,1)S(1)}, u32[]{:S(2)}, u32[]{:S(2)}) collective-permute-start(bf16[4,1008,128]{2,1,0:T(8,128)(2,1)S(1)} %shard_map.66.ref.own_ref), channel_id=1, source_target_pairs={{4,8},{8,4},{12,16},{16,12},{20,24},{24,20},{28,32},{32,28},{36,40... | collective-permute-start | bytes 3096584 | tf_op jit(solution)/shard_map/ppermute | solution.py:23
  29.5 3.5 %all-to-all-start.1 = ((bf16[4,624,128]{2,1,0:T(8,128)(2,1)}), bf16[4,624,128]{2,1,0:T(8,128)(2,1)S(1)}, u32[]{:S(2)}, u32[]{:S(2)}) async-start(bf16[4,624,128]{2,1,0:T(8,128)(2,1)} %shard_map.65.after_ref), calls=%async_computation.1 | async-start | bytes 1277952 | tf_op jit(solution)/shard_map/all_to_all | solution.py:27
  33.0 1.0 %shard_map.67 = (bf16[4,384,128]{2,1,0:T(8,128)(2,1)}, bf16[4,432,128]{2,1,0:T(8,128)(2,1)}, bf16[4,192,128]{2,1,0:T(8,128)(2,1)}) custom-call(bf16[4,1008,128]{2,1,0:T(8,128)(2,1)S(1)} %shard_map.66.ref.own_ref), custom_call_target="tpu_custom_call" | custom-call | tf_op jit(solution)/shard_map/pallas_call | solution.py:185
  34.0 1.9 %collective-permute-start.2 = (bf16[4,432,128]{2,1,0:T(8,128)(2,1)}, bf16[4,432,128]{2,1,0:T(8,128)(2,1)S(1)}, u32[]{:S(2)}, u32[]{:S(2)}) collective-permute-start(bf16[4,432,128]{2,1,0:T(8,128)(2,1)} %get-tuple-element.9), channel_id=1, source_target_pairs={{0,4},{4,0},{8,12},{12,8},{16,20},{20,16},{24,28},{28,24},{32,36},... | collective-permute-start | bytes 1327112 | tf_op jit(solution)/shard_map/ppermute | solution.py:23
  35.9 2.4 %collective-permute-start.1 = (bf16[4,384,128]{2,1,0:T(8,128)(2,1)}, bf16[4,384,128]{2,1,0:T(8,128)(2,1)S(1)}, u32[]{:S(2)}, u32[]{:S(2)}) collective-permute-start(bf16[4,384,128]{2,1,0:T(8,128)(2,1)} %get-tuple-element.8), channel_id=1, source_target_pairs={{0,4},{4,0},{8,12},{12,8},{16,20},{20,16},{24,28},{28,24},{32,36},... | collective-permute-start | bytes 1179656 | tf_op jit(solution)/shard_map/ppermute | solution.py:23
  38.3 1.9 %collective-permute-start.3 = (bf16[4,192,128]{2,1,0:T(8,128)(2,1)}, bf16[4,192,128]{2,1,0:T(8,128)(2,1)}, u32[]{:S(2)}, u32[]{:S(2)}) collective-permute-start(bf16[4,192,128]{2,1,0:T(8,128)(2,1)} %get-tuple-element.10), channel_id=1, source_target_pairs={{0,4},{4,0},{8,12},{12,8},{16,20},{20,16},{24,28},{28,24},{32,36},... | collective-permute-start | bytes 589832 | tf_op jit(solution)/shard_map/ppermute | solution.py:23
  40.9 2.1 %all-to-all-done.1.refs_3_ = bf16[4,624,128]{2,1,0:T(8,128)(2,1)S(1)} async-done(((bf16[4,624,128]{2,1,0:T(8,128)(2,1)}), bf16[4,624,128]{2,1,0:T(8,128)(2,1)S(1)}, u32[]{:S(2)}, u32[]{:S(2)}) %all-to-all-start.1) | async-done | bytes 639008 | tf_op jit(solution)/shard_map/all_to_all | solution.py:27
  43.0 0.0 collective-permute-done.3.refs_2_
  43.0 0.0 collective-permute-done.1.refs_0_
  43.0 0.0 collective-permute-done.2.refs_1_
  43.0 1.1 %collective-permute-done.across_ref = bf16[4,1008,128]{2,1,0:T(8,128)(2,1)S(1)} collective-permute-done((bf16[4,1008,128]{2,1,0:T(8,128)(2,1)S(1)}, bf16[4,1008,128]{2,1,0:T(8,128)(2,1)S(1)}, u32[]{:S(2)}, u32[]{:S(2)}) %collective-permute-start) | collective-permute-done | bytes 1032224 | tf_op jit(solution)/shard_map/ppermute | solution.py:23
  44.1 0.0 copy-done.1
  44.1 4.1 %shard_map.68 = f32[4,64,96]{2,1,0:T(8,128)S(1)} custom-call(s32[128]{0:T(128)S(1)} %copy-done.1, s32[1]{0:T(128)S(6)} %copy.7.step_ref, bf16[4,1008,128]{2,1,0:T(8,128)(2,1)S(1)} %shard_map.66.ref.own_ref, bf16[4,1008,128]{2,1,0:T(8,128)(2,1)S(1)} %collective-permute-done.across_ref, bf16[4,384,128]{2,1,0:T(8,128)(2,1)S(1)} %collective-permute-done.1.refs_0_, ...), custom_call_target="tpu_custom_call" | custom-call | flops 981467136 | bytes 3096576 | tf_op jit(solution)/shard_map/pallas_call | solution.py:279
  48.3 8.4 %all_to_all.15 = f32[4,64,96]{2,1,0:T(8,128)S(1)} all-to-all(f32[4,64,96]{2,1,0:T(8,128)S(1)} %shard_map.68), channel_id=1, replica_groups=mesh['seq'=128,'grp'=4] {'grp'}, dimensions={0} | all-to-all | bytes 196608 | tf_op jit(solution)/shard_map/all_to_all | solution.py:27
  56.7 0.6 %reduce_sum.9 = f32[64,96]{1,0:T(8,128)} reduce(f32[4,64,96]{2,1,0:T(8,128)S(1)} %all_to_all.15, f32[]{:T(128)} %constant.0.clone.1), dimensions={0}, to_apply=%region_0.0 | reduce | flops 18432 | bytes 122884 | tf_op jit(solution)/shard_map/reduce_sum | solution.py:309
Async XLA Ops:
  2.4 22.0 %all-to-all-start = ((bf16[4,1248,128]{2,1,0:T(8,128)(2,1)}), bf16[4,1248,128]{2,1,0:T(8,128)(2,1)S(1)}, u32[]{:S(2)}, u32[]{:S(2)}) async-start(bf16[4,1248,128]{2,1,0:T(8,128)(2,1)} %shard_map.64), calls=%async_computation | async-start | bytes 2555904 | tf_op jit(solution)/shard_map/all_to_all | solution.py:27
  6.9 17.6 %copy-start = (bf16[640,64]{0,1:T(8,128)(2,1)S(1)}, bf16[640,64]{0,1:T(8,128)(2,1)}, u32[]{:S(2)}) copy-start(bf16[640,64]{0,1:T(8,128)(2,1)} %param.8) | copy-start | bytes 245764
  24.9 19.3 %copy-start.1 = (s32[128]{0:T(128)S(1)}, s32[128]{0:T(128)}, u32[]{:S(2)}) copy-start(s32[128]{0:T(128)} %start_ref.1) | copy-start | bytes 1540
  24.9 19.3 %collective-permute-start = (bf16[4,1008,128]{2,1,0:T(8,128)(2,1)S(1)}, bf16[4,1008,128]{2,1,0:T(8,128)(2,1)S(1)}, u32[]{:S(2)}, u32[]{:S(2)}) collective-permute-start(bf16[4,1008,128]{2,1,0:T(8,128)(2,1)S(1)} %shard_map.66.ref.own_ref), channel_id=1, source_target_pairs={{4,8},{8,4},{12,16},{16,12},{20,24},{24,20},{28,32},{32,28},{36,40... | collective-permute-start | bytes 3096584 | tf_op jit(solution)/shard_map/ppermute | solution.py:23
  29.5 13.6 %all-to-all-start.1 = ((bf16[4,624,128]{2,1,0:T(8,128)(2,1)}), bf16[4,624,128]{2,1,0:T(8,128)(2,1)S(1)}, u32[]{:S(2)}, u32[]{:S(2)}) async-start(bf16[4,624,128]{2,1,0:T(8,128)(2,1)} %shard_map.65.after_ref), calls=%async_computation.1 | async-start | bytes 1277952 | tf_op jit(solution)/shard_map/all_to_all | solution.py:27
  34.0 9.1 %collective-permute-start.2 = (bf16[4,432,128]{2,1,0:T(8,128)(2,1)}, bf16[4,432,128]{2,1,0:T(8,128)(2,1)S(1)}, u32[]{:S(2)}, u32[]{:S(2)}) collective-permute-start(bf16[4,432,128]{2,1,0:T(8,128)(2,1)} %get-tuple-element.9), channel_id=1, source_target_pairs={{0,4},{4,0},{8,12},{12,8},{16,20},{20,16},{24,28},{28,24},{32,36},... | collective-permute-start | bytes 1327112 | tf_op jit(solution)/shard_map/ppermute | solution.py:23
  35.9 7.1 %collective-permute-start.1 = (bf16[4,384,128]{2,1,0:T(8,128)(2,1)}, bf16[4,384,128]{2,1,0:T(8,128)(2,1)S(1)}, u32[]{:S(2)}, u32[]{:S(2)}) collective-permute-start(bf16[4,384,128]{2,1,0:T(8,128)(2,1)} %get-tuple-element.8), channel_id=1, source_target_pairs={{0,4},{4,0},{8,12},{12,8},{16,20},{20,16},{24,28},{28,24},{32,36},... | collective-permute-start | bytes 1179656 | tf_op jit(solution)/shard_map/ppermute | solution.py:23
  38.3 4.7 %collective-permute-start.3 = (bf16[4,192,128]{2,1,0:T(8,128)(2,1)}, bf16[4,192,128]{2,1,0:T(8,128)(2,1)}, u32[]{:S(2)}, u32[]{:S(2)}) collective-permute-start(bf16[4,192,128]{2,1,0:T(8,128)(2,1)} %get-tuple-element.10), channel_id=1, source_target_pairs={{0,4},{4,0},{8,12},{12,8},{16,20},{20,16},{24,28},{28,24},{32,36},... | collective-permute-start | bytes 589832 | tf_op jit(solution)/shard_map/ppermute | solution.py:23

commit v5 on v4

--- a/solution.py
+++ b/solution.py
@@ -263,7 +263,7 @@
             w = 1.0 + 2.0 * step_ref[0].astype(jnp.float32) / 999.0
             for j in range(groups):
                 part = slice(j * tok, (j + 1) * tok)
-                out_ref[j] = (w * main[part] + (1.0 - w) * (whole[part] + shared[j])).T
+                out_ref[j] = (w * main[part] + (1.0 - w) * (whole[part] + shared[j])).T.astype(jnp.bfloat16)
 
         use_beside = (start_ref[tile] == tile) == (lax.rem(tile, 2) == 0)
 
@@ -278,7 +278,7 @@
     flops = int(4 * (heads + 1.5) * groups * tok * 2 * groups * tok * HD)
     return pl.pallas_call(
         kernel,
-        out_shape=jax.ShapeDtypeStruct((groups, half, tok), jnp.float32),
+        out_shape=jax.ShapeDtypeStruct((groups, half, tok), jnp.bfloat16),
         in_specs=[SMEM] * 2 + [VMEM] * (3 + len(beside)),
         out_specs=VMEM,
         scratch_shapes=[
@@ -306,7 +306,7 @@
     beside = [traded(part, "seq", 0) for part in cut(own, (0, 4 * tok, own.shape[1] - 2 * tok, own.shape[1]))]
     queries = swapped(packed)
     part = attention(window_start, timestep, own, across, beside, queries, heads, tok, half)
-    return jnp.sum(swapped(part), axis=0).T
+    return jnp.sum(swapped(part).astype(jnp.float32), axis=0).T
 
 
 def solution(mesh):

time: 57.7 us -> 57.4 us (level)
  no operation moved by 1% of the time
where the time goes in v5:
time: 57.4 us; the launch traced here: 56.9 us
  starting transfers between devices  18.8 us (33%)
  waiting for transfers between devices  18.7 us (33%)
  Pallas kernels  9.96 us (17%)
  blocking collectives  8.06 us (14%)
  between operations  0.74 us (1%)
  other arithmetic  0.63 us (1%)
    all_to_all x2, waiting for transfers between devices, swapped(): return lax.all_to_all(block, 'grp', 0, 0)  17.6 us
    ppermute x4, starting transfers between devices, traded(): lax.ppermute(block, axis, [p for i in lows for p in ((i, i + 1), (i + 1,...  10.8 us
    all_to_all x1, blocking collectives, swapped(): return lax.all_to_all(block, 'grp', 0, 0)  8.06 us
    all_to_all x2, starting transfers between devices, swapped(): return lax.all_to_all(block, 'grp', 0, 0)  7.97 us
    pallas_call x1, Pallas kernels, attention(): pl.pallas_call(kernel, out_shape=jax.ShapeDtypeStruct((groups, half, tok)...  4.1 us
    pallas_call x1, Pallas kernels, pack_keys(): pl.pallas_call(kernel, out_shape=jax.ShapeDtypeStruct((groups, rows, HD),...  2.42 us
    pallas_call x1, Pallas kernels, pack_queries(): pl.pallas_call(kernel, out_shape=jax.ShapeDtypeStruct((groups, rows, HD),...  2.05 us
  transfers between devices with their start and end apart: 6, of which 3 were waited for; matrix products, arithmetic and copies ran while one was open for 0% of the time, Pallas kernels for 5%

profile of v5, /device:TPU:384, one launch (start us, length us, event | category | flops | bytes accessed | tf_op | source)
XLA Modules:
  0.0 56.9 jit_solution(16422189837140425193)
XLA Ops:
  0.0 2.4 %shard_map.64 = bf16[4,1248,128]{2,1,0:T(8,128)(2,1)} custom-call(bf16[3,96,2560]{2,1,0:T(8,128)(2,1)} %bitcast.6, bf16[3,96,768]{2,1,0:T(8,128)(2,1)} %bitcast.8, bf16[64,768]{1,0:T(8,128)(2,1)} %bitcast.10), custom_call_target="tpu_custom_call" | custom-call | tf_op jit(solution)/shard_map/pallas_call | solution.py:91
  2.4 4.5 %all-to-all-start = ((bf16[4,1248,128]{2,1,0:T(8,128)(2,1)}), bf16[4,1248,128]{2,1,0:T(8,128)(2,1)S(1)}, u32[]{:S(2)}, u32[]{:S(2)}) async-start(bf16[4,1248,128]{2,1,0:T(8,128)(2,1)} %shard_map.64), calls=%async_computation | async-start | bytes 2555904 | tf_op jit(solution)/shard_map/all_to_all | solution.py:27
  6.9 0.0 copy-start
  6.9 2.0 %shard_map.65.after_ref = bf16[4,624,128]{2,1,0:T(8,128)(2,1)} custom-call(bf16[3,96,2560]{2,1,0:T(8,128)(2,1)} %bitcast.7, bf16[3,96,768]{2,1,0:T(8,128)(2,1)} %bitcast.9), custom_call_target="tpu_custom_call" | custom-call | tf_op jit(solution)/shard_map/pallas_call | solution.py:129
  9.0 15.5 %all-to-all-done.own_ref = bf16[4,1248,128]{2,1,0:T(8,128)(2,1)S(1)} async-done(((bf16[4,1248,128]{2,1,0:T(8,128)(2,1)}), bf16[4,1248,128]{2,1,0:T(8,128)(2,1)S(1)}, u32[]{:S(2)}, u32[]{:S(2)}) %all-to-all-start) | async-done | bytes 1277984 | tf_op jit(solution)/shard_map/all_to_all | solution.py:27
  24.5 0.0 copy-done
  24.5 0.4 shard_map.66.ref.own_ref
  24.9 0.0 copy-start.1
  24.9 4.6 %collective-permute-start = (bf16[4,1008,128]{2,1,0:T(8,128)(2,1)S(1)}, bf16[4,1008,128]{2,1,0:T(8,128)(2,1)S(1)}, u32[]{:S(2)}, u32[]{:S(2)}) collective-permute-start(bf16[4,1008,128]{2,1,0:T(8,128)(2,1)S(1)} %shard_map.66.ref.own_ref), channel_id=1, source_target_pairs={{4,8},{8,4},{12,16},{16,12},{20,24},{24,20},{28,32},{32,28},{36,40... | collective-permute-start | bytes 3096584 | tf_op jit(solution)/shard_map/ppermute | solution.py:23
  29.5 3.5 %all-to-all-start.1 = ((bf16[4,624,128]{2,1,0:T(8,128)(2,1)}), bf16[4,624,128]{2,1,0:T(8,128)(2,1)S(1)}, u32[]{:S(2)}, u32[]{:S(2)}) async-start(bf16[4,624,128]{2,1,0:T(8,128)(2,1)} %shard_map.65.after_ref), calls=%async_computation.1 | async-start | bytes 1277952 | tf_op jit(solution)/shard_map/all_to_all | solution.py:27
  33.0 1.0 %shard_map.67 = (bf16[4,384,128]{2,1,0:T(8,128)(2,1)}, bf16[4,432,128]{2,1,0:T(8,128)(2,1)}, bf16[4,192,128]{2,1,0:T(8,128)(2,1)}) custom-call(bf16[4,1008,128]{2,1,0:T(8,128)(2,1)S(1)} %shard_map.66.ref.own_ref), custom_call_target="tpu_custom_call" | custom-call | tf_op jit(solution)/shard_map/pallas_call | solution.py:185
  34.0 1.9 %collective-permute-start.2 = (bf16[4,432,128]{2,1,0:T(8,128)(2,1)}, bf16[4,432,128]{2,1,0:T(8,128)(2,1)S(1)}, u32[]{:S(2)}, u32[]{:S(2)}) collective-permute-start(bf16[4,432,128]{2,1,0:T(8,128)(2,1)} %get-tuple-element.9), channel_id=1, source_target_pairs={{0,4},{4,0},{8,12},{12,8},{16,20},{20,16},{24,28},{28,24},{32,36},... | collective-permute-start | bytes 1327112 | tf_op jit(solution)/shard_map/ppermute | solution.py:23
  35.9 2.4 %collective-permute-start.1 = (bf16[4,384,128]{2,1,0:T(8,128)(2,1)}, bf16[4,384,128]{2,1,0:T(8,128)(2,1)S(1)}, u32[]{:S(2)}, u32[]{:S(2)}) collective-permute-start(bf16[4,384,128]{2,1,0:T(8,128)(2,1)} %get-tuple-element.8), channel_id=1, source_target_pairs={{0,4},{4,0},{8,12},{12,8},{16,20},{20,16},{24,28},{28,24},{32,36},... | collective-permute-start | bytes 1179656 | tf_op jit(solution)/shard_map/ppermute | solution.py:23
  38.3 1.9 %collective-permute-start.3 = (bf16[4,192,128]{2,1,0:T(8,128)(2,1)}, bf16[4,192,128]{2,1,0:T(8,128)(2,1)}, u32[]{:S(2)}, u32[]{:S(2)}) collective-permute-start(bf16[4,192,128]{2,1,0:T(8,128)(2,1)} %get-tuple-element.10), channel_id=1, source_target_pairs={{0,4},{4,0},{8,12},{12,8},{16,20},{20,16},{24,28},{28,24},{32,36},... | collective-permute-start | bytes 589832 | tf_op jit(solution)/shard_map/ppermute | solution.py:23
  40.9 2.1 %all-to-all-done.1.refs_3_ = bf16[4,624,128]{2,1,0:T(8,128)(2,1)S(1)} async-done(((bf16[4,624,128]{2,1,0:T(8,128)(2,1)}), bf16[4,624,128]{2,1,0:T(8,128)(2,1)S(1)}, u32[]{:S(2)}, u32[]{:S(2)}) %all-to-all-start.1) | async-done | bytes 639008 | tf_op jit(solution)/shard_map/all_to_all | solution.py:27
  43.0 0.0 collective-permute-done.3.refs_2_
  43.0 0.0 collective-permute-done.1.refs_0_
  43.0 0.0 collective-permute-done.2.refs_1_
  43.0 1.1 %collective-permute-done.across_ref = bf16[4,1008,128]{2,1,0:T(8,128)(2,1)S(1)} collective-permute-done((bf16[4,1008,128]{2,1,0:T(8,128)(2,1)S(1)}, bf16[4,1008,128]{2,1,0:T(8,128)(2,1)S(1)}, u32[]{:S(2)}, u32[]{:S(2)}) %collective-permute-start) | collective-permute-done | bytes 1032224 | tf_op jit(solution)/shard_map/ppermute | solution.py:23
  44.1 0.0 copy-done.1
  44.1 4.1 %shard_map.68 = bf16[4,64,96]{2,1,0:T(8,128)(2,1)S(1)} custom-call(s32[128]{0:T(128)S(1)} %copy-done.1, s32[1]{0:T(128)S(6)} %copy.7.step_ref, bf16[4,1008,128]{2,1,0:T(8,128)(2,1)S(1)} %shard_map.66.ref.own_ref, bf16[4,1008,128]{2,1,0:T(8,128)(2,1)S(1)} %collective-permute-done.across_ref, bf16[4,384,128]{2,1,0:T(8,128)(2,1)S(1)} %collective-permute-done.1.refs_0_, ...), custom_call_target="tpu_custom_call" | custom-call | flops 981467136 | bytes 3096576 | tf_op jit(solution)/shard_map/pallas_call | solution.py:279
  48.2 8.1 %all_to_all.15 = bf16[4,64,96]{2,1,0:T(8,128)(2,1)S(1)} all-to-all(bf16[4,64,96]{2,1,0:T(8,128)(2,1)S(1)} %shard_map.68), channel_id=1, replica_groups=mesh['seq'=128,'grp'=4] {'grp'}, dimensions={0} | all-to-all | bytes 98304 | tf_op jit(solution)/shard_map/all_to_all | solution.py:27
  56.3 0.6 %convert_reduce_fusion = f32[64,96]{1,0:T(8,128)} fusion(bf16[4,64,96]{2,1,0:T(8,128)(2,1)S(1)} %all_to_all.15), kind=kLoop, calls=%fused_computation | loop fusion | flops 43008 | bytes 73728 | tf_op jit(solution)/shard_map/reduce_sum | solution.py:309
Async XLA Ops:
  2.4 22.0 %all-to-all-start = ((bf16[4,1248,128]{2,1,0:T(8,128)(2,1)}), bf16[4,1248,128]{2,1,0:T(8,128)(2,1)S(1)}, u32[]{:S(2)}, u32[]{:S(2)}) async-start(bf16[4,1248,128]{2,1,0:T(8,128)(2,1)} %shard_map.64), calls=%async_computation | async-start | bytes 2555904 | tf_op jit(solution)/shard_map/all_to_all | solution.py:27
  6.9 17.6 %copy-start = (bf16[640,64]{0,1:T(8,128)(2,1)S(1)}, bf16[640,64]{0,1:T(8,128)(2,1)}, u32[]{:S(2)}) copy-start(bf16[640,64]{0,1:T(8,128)(2,1)} %param.8) | copy-start | bytes 245764
  24.9 19.3 %copy-start.1 = (s32[128]{0:T(128)S(1)}, s32[128]{0:T(128)}, u32[]{:S(2)}) copy-start(s32[128]{0:T(128)} %start_ref.1) | copy-start | bytes 1540
  24.9 19.3 %collective-permute-start = (bf16[4,1008,128]{2,1,0:T(8,128)(2,1)S(1)}, bf16[4,1008,128]{2,1,0:T(8,128)(2,1)S(1)}, u32[]{:S(2)}, u32[]{:S(2)}) collective-permute-start(bf16[4,1008,128]{2,1,0:T(8,128)(2,1)S(1)} %shard_map.66.ref.own_ref), channel_id=1, source_target_pairs={{4,8},{8,4},{12,16},{16,12},{20,24},{24,20},{28,32},{32,28},{36,40... | collective-permute-start | bytes 3096584 | tf_op jit(solution)/shard_map/ppermute | solution.py:23
  29.5 13.6 %all-to-all-start.1 = ((bf16[4,624,128]{2,1,0:T(8,128)(2,1)}), bf16[4,624,128]{2,1,0:T(8,128)(2,1)S(1)}, u32[]{:S(2)}, u32[]{:S(2)}) async-start(bf16[4,624,128]{2,1,0:T(8,128)(2,1)} %shard_map.65.after_ref), calls=%async_computation.1 | async-start | bytes 1277952 | tf_op jit(solution)/shard_map/all_to_all | solution.py:27
  34.0 9.1 %collective-permute-start.2 = (bf16[4,432,128]{2,1,0:T(8,128)(2,1)}, bf16[4,432,128]{2,1,0:T(8,128)(2,1)S(1)}, u32[]{:S(2)}, u32[]{:S(2)}) collective-permute-start(bf16[4,432,128]{2,1,0:T(8,128)(2,1)} %get-tuple-element.9), channel_id=1, source_target_pairs={{0,4},{4,0},{8,12},{12,8},{16,20},{20,16},{24,28},{28,24},{32,36},... | collective-permute-start | bytes 1327112 | tf_op jit(solution)/shard_map/ppermute | solution.py:23
  35.9 7.1 %collective-permute-start.1 = (bf16[4,384,128]{2,1,0:T(8,128)(2,1)}, bf16[4,384,128]{2,1,0:T(8,128)(2,1)S(1)}, u32[]{:S(2)}, u32[]{:S(2)}) collective-permute-start(bf16[4,384,128]{2,1,0:T(8,128)(2,1)} %get-tuple-element.8), channel_id=1, source_target_pairs={{0,4},{4,0},{8,12},{12,8},{16,20},{20,16},{24,28},{28,24},{32,36},... | collective-permute-start | bytes 1179656 | tf_op jit(solution)/shard_map/ppermute | solution.py:23
  38.3 4.7 %collective-permute-start.3 = (bf16[4,192,128]{2,1,0:T(8,128)(2,1)}, bf16[4,192,128]{2,1,0:T(8,128)(2,1)}, u32[]{:S(2)}, u32[]{:S(2)}) collective-permute-start(bf16[4,192,128]{2,1,0:T(8,128)(2,1)} %get-tuple-element.10), channel_id=1, source_target_pairs={{0,4},{4,0},{8,12},{12,8},{16,20},{20,16},{24,28},{28,24},{32,36},... | collective-permute-start | bytes 589832 | tf_op jit(solution)/shard_map/ppermute | solution.py:23
